TPU v7x, 128 devices: a whole 4x4x4 slice. The times are simulated.
128 devices in a mesh: dom: 32 (over y, x, core), esplit: 4 (over z).
Axes of the slice: x: 4, y: 4, z: 4, core: 2. Of those that a mesh axis runs over, the one named last changes fastest.
Arguments:
- features: bfloat16 [524288, 128], P('dom'), may hold values from -6 to 6
- adjacency: bfloat16 [32, 4, 16, 128, 32, 128], P('dom', 'esplit'), as said below
- tile_source: int32 [32, 4, 16, 32], P('dom', 'esplit'), may hold values from 0 to 287, as said below
- hub_rows: int32 [32, 512], P('dom'), may hold values from 0 to 16383, as said below
- send_rows: int32 [32, 32, 128], P('dom'), may hold values from 0 to 16383, as said below
- send_live: int32 [32, 32], P('dom'), may hold values from 32 to 128, as said below
- target_block: int32 [32], P('dom'), may hold values from 0 to 112
- w_self: bfloat16 [128, 128], replicated, may hold values from -0.5 to 0.5
- w_neigh: bfloat16 [128, 128], replicated, may hold values from -2 to 2
- out_bias: bfloat16 [128], replicated, may hold values from -3 to 3
- out_grad: bfloat16 [65536, 128], P('dom'), may hold values from -6 to 6
Outputs:
- layer_out: bfloat16 [65536, 128], P(('dom', 'esplit'))
- grad_features: float32 [524288, 128], P(('dom', 'esplit'))
- grad_w_self: float32 [128, 128], replicated
- grad_w_neigh: float32 [128, 128], replicated
- grad_bias: float32 [128], replicated
Inputs may be any that keep to these rules, and one draw needn't show every extreme that they name: `adjacency`: nonnegative edge weights, zero where a tile holds no edge. `tile_source`: a block index into the partition's source table. `hub_rows`: distinct local rows within each partition. `send_rows`: local rows of the sending partition, distinct within each list. `send_live`: in each sender's lists one reaches 128.
All inputs are finite; a program needn't handle non-finite values.
Results may differ from a plain program's by a relative error of at most 0.00045.
Values may be sent and summed in bfloat16 or wider, within the bound.
A program may use at most 256 MiB of HBM per device.

v0:
```python
import math

import jax
import jax.numpy as jnp
from jax import lax
from jax.sharding import PartitionSpec as P


def boundary_packet(hub_part, halo_part, peer_count, split_count, hub_count):
    feat_width = hub_part.shape[-1]
    hub_quarter = hub_count // split_count
    hub_split = jnp.broadcast_to(
        hub_part.reshape(-1, split_count, hub_quarter, feat_width),
        (peer_count, split_count, hub_quarter, feat_width),
    )
    halo_split = halo_part.reshape(peer_count, split_count, -1, feat_width)
    return jnp.concatenate([hub_split, halo_split], axis=2)


def local(
    features,
    adjacency,
    tile_source,
    hub_rows,
    send_rows,
    send_live,
    target_block,
    w_self,
    w_neigh,
    out_bias,
    out_grad,
):
    highest = lax.Precision.HIGHEST
    own_count, feat_width = features.shape
    peer_count = lax.axis_size("dom")
    split_count = lax.axis_size("esplit")
    split_index = lax.axis_index("esplit")
    tile_vals = adjacency[0, 0]
    tile_blocks = tile_source[0, 0]
    target_blocks, tile_rows, slot_count, _ = tile_vals.shape
    target_count = target_blocks * tile_rows
    quarter_rows = target_count // split_count
    hub_local_rows = hub_rows[0]
    hub_count = hub_local_rows.shape[0]
    hub_quarter = hub_count // split_count
    halo_lists = send_rows[0]
    halo_count = halo_lists.shape[1]
    live_slots = jnp.arange(halo_count, dtype=jnp.int32)[None, :] < send_live[0][:, None]
    hub_local = features[hub_local_rows]
    halo_send = jnp.where(
        live_slots[:, :, None], features[halo_lists], jnp.zeros((), features.dtype)
    )
    w_neigh_wide = w_neigh.astype(jnp.float32)
    packet = boundary_packet(hub_local, halo_send, peer_count, split_count, hub_count)
    arrived = lax.all_to_all(packet, "dom", split_axis=0, concat_axis=0, tiled=True)
    hub_table = arrived[:, :, :hub_quarter].reshape(peer_count * hub_count, feat_width)
    halo_table = arrived[:, :, hub_quarter:].reshape(peer_count * halo_count, feat_width)
    source_table = jnp.concatenate([features, hub_table, halo_table], axis=0)
    table_blocks = source_table.shape[0] // tile_rows
    gathered = source_table.reshape(table_blocks, tile_rows, feat_width)[tile_blocks]
    numerator = jnp.einsum(
        "bikj,bkjf->bif", tile_vals, gathered, preferred_element_type=jnp.float32
    ).reshape(target_count, feat_width)
    degree = jnp.sum(tile_vals, axis=(2, 3), dtype=jnp.float32).reshape(target_count)
    start_row = target_block[0] * tile_rows
    quarter_start = split_index * quarter_rows
    self_start = start_row + quarter_start
    self_rows = lax.dynamic_slice_in_dim(features, self_start, quarter_rows, 0)
    grad_rows = lax.dynamic_slice_in_dim(out_grad, quarter_start, quarter_rows, 0)
    grad_rows_wide = grad_rows.astype(jnp.float32)
    numer_total, degree_total = lax.psum((numerator, degree), "esplit")
    divisor = jnp.maximum(degree_total, 1.0)[:, None]
    aggregate = lax.dynamic_slice_in_dim(
        numer_total, quarter_start, quarter_rows, 0
    ) / lax.dynamic_slice_in_dim(divisor, quarter_start, quarter_rows, 0)
    numer_grad = jnp.dot(out_grad.astype(jnp.float32), w_neigh_wide.T, precision=highest) / divisor
    layer_out = (
        jnp.dot(aggregate, w_neigh_wide, precision=highest)
        + jnp.dot(self_rows, w_self, preferred_element_type=jnp.float32)
        + out_bias.astype(jnp.float32)
    ).astype(jnp.bfloat16)
    contract = (((0,), (0,)), ((), ()))
    self_wgrad, neigh_wgrad, bias_grad = lax.psum(
        (
            lax.dot_general(self_rows, grad_rows, contract, preferred_element_type=jnp.float32),
            lax.dot_general(aggregate, grad_rows_wide, contract, precision=highest),
            jnp.sum(grad_rows_wide, axis=0),
        ),
        ("dom", "esplit"),
    )
    total_scale = math.sqrt(quarter_rows * split_count * peer_count)
    contrib = jnp.einsum(
        "bikj,bif->bkjf",
        tile_vals.astype(jnp.float32),
        numer_grad.reshape(target_blocks, tile_rows, feat_width),
        precision=highest,
    )
    grad_table = (
        jnp.zeros((table_blocks, tile_rows, feat_width), jnp.float32)
        .at[tile_blocks]
        .add(contrib)
        .reshape(-1, feat_width)
    )
    own_grad = grad_table[:own_count]
    hub_grad = grad_table[own_count : own_count + peer_count * hub_count]
    halo_grad = grad_table[own_count + peer_count * hub_count :].reshape(
        peer_count, halo_count, feat_width
    )
    self_grad = lax.dynamic_slice_in_dim(own_grad, self_start, quarter_rows, 0) + jnp.dot(
        grad_rows, w_self.T, preferred_element_type=jnp.float32
    )
    own_grad = lax.dynamic_update_slice_in_dim(own_grad, self_grad, self_start, 0)
    grad_packet = boundary_packet(hub_grad, halo_grad, peer_count, split_count, hub_count)
    returned = lax.all_to_all(grad_packet, "dom", split_axis=0, concat_axis=0, tiled=True)
    own_grad = own_grad.at[hub_local_rows].add(
        jnp.sum(returned[:, :, :hub_quarter], axis=0).reshape(hub_count, feat_width)
    )
    halo_back = returned[:, :, hub_quarter:].reshape(peer_count, halo_count, feat_width)
    own_grad = own_grad.at[halo_lists].add(jnp.where(live_slots[:, :, None], halo_back, 0.0))
    grad_features = lax.psum_scatter(own_grad, "esplit", scatter_dimension=0, tiled=True)
    return (
        layer_out,
        grad_features,
        self_wgrad / total_scale,
        neigh_wgrad / total_scale,
        bias_grad / total_scale,
    )


def solution(mesh):
    in_specs = (
        P("dom", None),
        P("dom", "esplit", None, None, None, None),
        P("dom", "esplit", None, None),
        P("dom", None),
        P("dom", None, None),
        P("dom", None),
        P("dom"),
        P(),
        P(),
        P(),
        P("dom", None),
    )
    out_specs = (P(("dom", "esplit"), None), P(("dom", "esplit"), None), P(), P(), P())
    return jax.shard_map(local, mesh=mesh, in_specs=in_specs, out_specs=out_specs, check_vma=False)
```

profile of v0, /device:TPU:0, one launch (start us, length us, event | category | flops | bytes accessed | tf_op | source)
XLA Modules:
  0.0 645.3 jit_solution(12707456494024969484)
XLA Ops:
  7.2 0.0 copy-start
  7.2 0.0 copy-start.5
  7.2 0.7 compare_select_fusion.2
  7.9 0.7 broadcast_clamp_fusion
  8.6 3.8 gather_fusion
  12.4 13.8 %gather_fusion.1 = bf16[4096,128]{1,0:T(8,128)(2,1)S(1)} fusion(bf16[16384,128]{1,0:T(8,128)(2,1)} %param.11, s32[4096]{0:T(1024)S(1)} %broadcast_clamp_fusion), kind=kCustom, calls=%fused_computation.1 | custom fusion | bytes 2113536 | tf_op jit(solution)/shard_map/gather | solution.py:51
  26.2 0.0 copy-done.5
  26.2 0.1 broadcast_compare_fusion
  26.3 0.7 broadcast_select_fusion
  27.0 1.0 broadcast_in_dim.46
  28.1 0.0 copy-start.4
  28.1 2.8 pad_maximum_fusion.2
  30.9 7.5 %all-to-all-start = ((bf16[32,4,160,128]{3,2,1,0:T(8,128)(2,1)}), bf16[32,4,160,128]{3,2,1,0:T(8,128)(2,1)}, u32[]{:S(2)}, u32[]{:S(2)}) async-start(bf16[32,4,160,128]{3,2,1,0:T(8,128)(2,1)} %pad_maximum_fusion.2), calls=%async_computation | async-start | bytes 10485760 | tf_op jit(solution)/shard_map/all_to_all | solution.py:55
  38.4 0.0 copy-done.4
  38.4 0.0 copy-start.2
  38.4 0.0 copy-start.6
  38.4 0.1 reshape.197
  38.5 17.5 %convert_reduce_fusion = f32[16,128]{1,0:T(8,128)S(1)} fusion(bf16[1,1,16,128,32,128]{5,4,3,2,1,0:T(8,128)(2,1)} %param.12), kind=kLoop, calls=%fused_computation.6 | loop fusion | flops 16775168 | bytes 16785408 | tf_op jit(solution)/shard_map/reduce_sum | solution.py:64
  56.0 11.9 %psum.36 = f32[2048]{0:T(1024)S(1)} all-reduce(f32[2048]{0:T(1024)S(1)} %bitcast.70), channel_id=1, replica_groups=mesh['dom'=32,'esplit'=4] {'esplit'}, use_global_device_ids=true, to_apply=%region_2.3 | all-reduce | flops 2048 | bytes 16384 | tf_op jit(solution)/shard_map/psum | solution.py:71
  67.9 0.0 copy-done.2
  67.9 0.0 copy-done.6
  67.9 0.4 convolution_divide_fusion
  68.3 29.1 %fusion = f32[16,128,32,128]{3,1,2,0:T(8,128)} fusion(f32[16,128,128,1]{2,1,3,0:T(8,128)S(1)} %bitcast.66, bf16[16,128,32,128]{3,2,1,0:T(8,128)(2,1)} %bitcast.56), kind=kOutput, calls=%fused_computation.7 | convolution fusion | flops 12884901888 | bytes 51380224 | tf_op jit(solution)/shard_map/bikj,bif->bkjf/dot_general | solution.py:92
  97.4 33.4 %copy.22 = f32[512,128,128]{2,1,0:T(8,128)} copy(f32[512,128,128]{1,2,0:T(8,128)} %bitcast.54) | data formatting | bytes 67108864 | tf_op jit(solution)/shard_map/bikj,bif->bkjf/dot_general | solution.py:92
  130.8 8.9 %broadcast_in_dim.49 = f32[288,128,128]{2,1,0:T(8,128)} broadcast(f32[]{:T(128)} %constant.7.clone.1), dimensions={} | broadcast | bytes 18874372 | tf_op jit(solution)/shard_map/broadcast_in_dim | solution.py:99
  139.7 103.5 %scatter_fusion = f32[288,128,128]{2,1,0:T(8,128)} fusion(f32[288,128,128]{2,1,0:T(8,128)} %broadcast_in_dim.49, s32[512]{0:T(512)S(1)} %reshape.197, f32[512,128,128]{2,1,0:T(8,128)} %copy.22), kind=kCustom, calls=%fused_computation.3 | custom fusion | flops 8388608 | bytes 100665344 | tf_op jit(solution)/shard_map/scatter-add | solution.py:101
  243.2 1.7 slice.44
  244.9 11.3 %fusion.21 = (f32[128,128,128]{2,1,0:T(8,128)}, f32[128,128,128]{2,1,0:T(8,128)}) fusion(f32[288,128,128]{2,1,0:T(8,128)} %scatter_fusion), kind=kLoop, calls=%fused_computation.52 | loop fusion | bytes 33554432 | tf_op jit(solution)/shard_map/slice | solution.py:105
  256.2 8.4 %pad_maximum_fusion = f32[32,4,160,128]{3,2,1,0:T(8,128)} fusion(f32[32,4,32,128]{3,2,1,0:T(8,128)S(1)} %bitcast.63, f32[32,4,128,128]{3,2,1,0:T(8,128)} %bitcast.59), kind=kLoop, calls=%fused_computation.11 | loop fusion | flops 2621440 | bytes 20971520 | tf_op jit(solution)/shard_map/concatenate | solution.py:17
  264.6 0.0 all-to-all-done
  264.6 7.6 %all-to-all-start.1 = ((f32[32,4,160,128]{3,2,1,0:T(8,128)}), f32[32,4,160,128]{3,2,1,0:T(8,128)}, u32[]{:S(2)}, u32[]{:S(2)}) async-start(f32[32,4,160,128]{3,2,1,0:T(8,128)} %pad_maximum_fusion), calls=%async_computation.1 | async-start | bytes 20971520 | tf_op jit(solution)/shard_map/all_to_all | solution.py:114
  272.2 0.0 all-reduce.4.cloned.1.call-start
  272.2 0.0 copy-start.1
  272.3 2.7 slice.40
  274.9 1.3 slice.41
  276.3 0.0 copy-done.1
  276.3 54.8 %pad_maximum_fusion.1 = bf16[36864,128]{1,0:T(8,128)(2,1)} fusion(bf16[4096,128]{1,0:T(8,128)(2,1)S(1)} %bitcast.65, bf16[16384,128]{1,0:T(8,128)(2,1)S(1)} %bitcast.61, bf16[16384,128]{1,0:T(8,128)(2,1)S(1)} %copy-done.1), kind=kLoop, calls=%fused_computation.12 | loop fusion | flops 28311552 | bytes 18874368 | tf_op jit(solution)/shard_map/concatenate | solution.py:58
  331.1 17.7 %gather_fusion.2 = bf16[512,128,128]{2,1,0:T(8,128)(2,1)} fusion(bf16[288,128,128]{2,1,0:T(8,128)(2,1)} %bitcast.58, s32[1024]{0:T(1024)S(1)} %pad_clamp_fusion), kind=kCustom, calls=%fused_computation.2 | custom fusion | bytes 33556480 | tf_op jit(solution)/shard_map/gather | solution.py:60
  348.8 15.8 %fusion.2 = f32[16,128,128,1]{1,2,3,0:T(8,128)} fusion(bf16[16,32,128,128]{3,2,1,0:T(8,128)(2,1)} %bitcast.60, bf16[16,128,32,128]{3,2,1,0:T(8,128)(2,1)} %bitcast.57), kind=kOutput, calls=%fused_computation.9 | convolution fusion | flops 2147483648 | bytes 34603008 | tf_op jit(solution)/shard_map/bikj,bkjf->bif/dot_general | solution.py:61
  364.6 0.0 all-reduce.4.cloned.1.call-update
  364.6 0.0 all-reduce.6.cloned.1.call-start
  364.7 0.1 dynamic-slice.3
  365.4 1.8 fusion.7
  367.2 0.1 iota_compare_fusion
  367.3 1.8 fusion.4
  369.1 41.0 %all-reduce.4.cloned.1.call-done = f32[2048,128]{1,0:T(8,128)} async-done(((f32[2048,128]{1,0:T(8,128)}), f32[2048,128]{1,0:T(8,128)}) %all-reduce.4.cloned.1.call-update) | async-done | bytes 1048592 | tf_op jit(solution)/shard_map/psum | solution.py:71
  410.1 2.1 fusion.10
  412.2 0.0 all-reduce.6.cloned.1.call-update
  412.2 0.0 reduce-scatter.2.cloned.1.call-start
  412.2 0.0 all-to-all-done.1
  412.3 3.8 slice_reduce_fusion
  416.1 1.8 slice.46
  417.9 0.9 bitcast_select_fusion
  418.8 9.7 %scatter_fusion.1 = f32[16384,128]{1,0:T(8,128)} fusion(f32[16384,128]{1,0:T(8,128)} %fusion.4, s32[512]{0:T(512)S(1)} %bitcast.72, f32[512,128]{1,0:T(8,128)S(1)} %bitcast.67), kind=kCustom, calls=%fused_computation.4 | custom fusion | flops 65536 | bytes 788480 | tf_op jit(solution)/shard_map/scatter-add | solution.py:115
  428.5 27.0 %scatter_fusion.2 = f32[16384,128]{1,0:T(8,128)} fusion(f32[16384,128]{1,0:T(8,128)} %scatter_fusion.1, s32[4096]{0:T(1024)S(1)} %fusion.15, f32[4096,128]{1,0:T(8,128)S(1)} %bitcast.62), kind=kCustom, calls=%fused_computation.5 | custom fusion | flops 524288 | bytes 6307840 | tf_op jit(solution)/shard_map/scatter-add | solution.py:119
  455.5 0.0 reduce-scatter.2.cloned.1.call-update
  455.5 0.1 convert_reduce_fusion.1
  455.6 64.9 %psum.39 = f32[128]{0:T(128)S(1)} all-reduce(f32[128]{0:T(128)S(1)} %convert_reduce_fusion.1), channel_id=1, replica_groups=mesh['dom'=32,'esplit'=4] {'dom','esplit'}, use_global_device_ids=true, to_apply=%region_11.12 | all-reduce | flops 128 | bytes 1024 | tf_op jit(solution)/shard_map/psum | solution.py:83
  520.6 0.5 broadcast_multiply_fusion.2
  521.1 1.3 fusion.14
  522.4 1.7 fusion.6
  524.1 33.5 %all-reduce.6.cloned.1.call-done = (f32[128,128]{1,0:T(8,128)}, f32[128,128]{1,0:T(8,128)}) async-done(((f32[128,128]{1,0:T(8,128)}, f32[128,128]{1,0:T(8,128)}), (f32[128,128]{1,0:T(8,128)}, f32[128,128]{1,0:T(8,128)})) %all-reduce.6.cloned.1.call-update) | async-done | bytes 131088 | tf_op jit(solution)/shard_map/psum | solution.py:83
  557.6 1.5 broadcast_multiply_fusion
  559.1 79.4 %reduce-scatter.2.cloned.1.call-done = f32[4096,128]{1,0:T(8,128)} async-done(((f32[16384,128]{1,0:T(8,128)}), f32[4096,128]{1,0:T(8,128)}) %reduce-scatter.2.cloned.1.call-update) | async-done | bytes 2097168 | tf_op jit(solution)/shard_map/reduce_scatter | solution.py:120
  (12 shorter events, 0.0 us)
Async XLA Ops:
  7.2 360.1 %copy-start = (bf16[128,128]{1,0:T(8,128)(2,1)S(1)}, bf16[128,128]{1,0:T(8,128)(2,1)}, u32[]{:S(2)}) copy-start(bf16[128,128]{1,0:T(8,128)(2,1)} %param.18) | copy-start | bytes 98308
  7.2 19.0 %copy-start.5 = (s32[1,32]{1,0:T(1,128)S(1)}, s32[1,32]{1,0:T(1,128)}, u32[]{:S(2)}) copy-start(s32[1,32]{1,0:T(1,128)} %param.16) | copy-start | bytes 388
  28.1 10.3 %copy-start.4 = (s32[1,1,16,32]{3,2,1,0:T(8,128)S(1)}, s32[1,1,16,32]{3,2,1,0:T(8,128)}, u32[]{:S(2)}) copy-start(s32[1,1,16,32]{3,2,1,0:T(8,128)} %param.13) | copy-start | bytes 6148
  30.9 233.7 %all-to-all-start = ((bf16[32,4,160,128]{3,2,1,0:T(8,128)(2,1)}), bf16[32,4,160,128]{3,2,1,0:T(8,128)(2,1)}, u32[]{:S(2)}, u32[]{:S(2)}) async-start(bf16[32,4,160,128]{3,2,1,0:T(8,128)(2,1)} %pad_maximum_fusion.2), calls=%async_computation | async-start | bytes 10485760 | tf_op jit(solution)/shard_map/all_to_all | solution.py:55
  38.4 29.5 %copy-start.2 = (bf16[2048,128]{1,0:T(8,128)(2,1)S(1)}, bf16[2048,128]{1,0:T(8,128)(2,1)}, u32[]{:S(2)}) copy-start(bf16[2048,128]{1,0:T(8,128)(2,1)} %param.21) | copy-start | bytes 1572868
  38.4 29.5 %copy-start.6 = (bf16[128,128]{1,0:T(8,128)(2,1)S(1)}, bf16[128,128]{1,0:T(8,128)(2,1)}, u32[]{:S(2)}) copy-start(bf16[128,128]{1,0:T(8,128)(2,1)} %param.19) | copy-start | bytes 98308
  264.6 147.7 %all-to-all-start.1 = ((f32[32,4,160,128]{3,2,1,0:T(8,128)}), f32[32,4,160,128]{3,2,1,0:T(8,128)}, u32[]{:S(2)}, u32[]{:S(2)}) async-start(f32[32,4,160,128]{3,2,1,0:T(8,128)} %pad_maximum_fusion), calls=%async_computation.1 | async-start | bytes 20971520 | tf_op jit(solution)/shard_map/all_to_all | solution.py:114
  272.2 137.9 %all-reduce.4.cloned.1.call-start = ((), (), s32[]{:S(2)}) async-start(), calls=%async_computation.3 | async-start | bytes 2097152 | tf_op jit(solution)/shard_map/psum | solution.py:71
  272.2 4.1 copy-start.1
  348.8 18.5 %copy-start.3 = (s32[1,32,128]{2,1,0:T(8,128)S(1)}, s32[1,32,128]{2,1,0:T(8,128)}, u32[]{:S(2)}) copy-start(s32[1,32,128]{2,1,0:T(8,128)} %param.15) | copy-start | bytes 49156
  364.6 193.0 %all-reduce.6.cloned.1.call-start = ((), (), s32[]{:S(2)}) async-start(), calls=%async_computation.5 | async-start | bytes 262144 | tf_op jit(solution)/shard_map/psum | solution.py:83
  412.2 226.3 %reduce-scatter.2.cloned.1.call-start = ((), (), s32[]{:S(2)}) async-start(), calls=%async_computation.4 | async-start | bytes 10485760 | tf_op jit(solution)/shard_map/reduce_scatter | solution.py:120
  428.5 27.0 %copy-start.7 = (bf16[128]{0:T(256)(128)(2,1)S(1)}, bf16[128]{0:T(256)(128)(2,1)}, u32[]{:S(2)}) copy-start(bf16[128]{0:T(256)(128)(2,1)} %param.20) | copy-start | bytes 772
Sparse Core Ops, SparseCore 0:
  364.7 45.2 all-reduce.3
  416.3 141.2 all-reduce.5
  560.6 77.8 reduce-scatter.1
where the time goes:
time: 653 us; the launch traced here: 645 us
  other arithmetic  233 us (36%)
  waiting for transfers between devices  154 us (24%)
  local copies, waits for them, and re-layouts  97.6 us (15%)
  blocking collectives  76.8 us (12%)
  matrix products  54 us (8%)
  starting transfers between devices  15.2 us (2%)
  between operations  14.9 us (2%)
    scatter-add x1, other arithmetic, local(): grad_table = jnp.zeros((table_blocks, tile_rows, feat_width), jnp.float32...  104 us
    reduce_scatter x1, waiting for transfers between devices, local(): lax.psum_scatter(own_grad, 'esplit', scatter_dimension=0, tiled=True)  79.4 us
    psum x1, blocking collectives, local(): lax.psum((lax.dot_general(self_rows, grad_rows, contract, preferred_eleme...  64.9 us
    concatenate x1, other arithmetic, local(): source_table = jnp.concatenate([features, hub_table, halo_table], axis=0)  54.8 us
    psum x1, waiting for transfers between devices, local(): numer_total, degree_total = lax.psum((numerator, degree), 'esplit')  41 us
    psum x1, waiting for transfers between devices, local(): lax.psum((lax.dot_general(self_rows, grad_rows, contract, preferred_eleme...  33.5 us
    dot_general x1, local copies, waits for them, and re-layouts, local(): jnp.einsum('bikj,bif->bkjf', tile_vals.astype(jnp.float32), numer_grad.re...  33.4 us
    dot_general x1, matrix products, local(): jnp.einsum('bikj,bif->bkjf', tile_vals.astype(jnp.float32), numer_grad.re...  29.1 us
  transfers between devices with their start and end apart: 5, of which 3 were waited for; matrix products, arithmetic and copies ran while one was open for 56% of the time, Pallas kernels for 0%

commit v1 on v0

v1 whole, which is shorter than its diff:
```python
import math

import jax
import jax.numpy as jnp
from jax import lax
from jax.experimental import pallas as pl
from jax.experimental.pallas import tpu as pltpu
from jax.sharding import PartitionSpec as P

F32 = jnp.float32
BF16 = jnp.bfloat16
VMEM_LIMIT = 56 * 2**20
ANY = pl.BlockSpec(memory_space=pl.ANY)
SMEM = pl.BlockSpec(memory_space=pltpu.SMEM)
VMEM = pl.BlockSpec(memory_space=pltpu.VMEM)
PARAMS = pltpu.CompilerParams(vmem_limit_bytes=VMEM_LIMIT)


def block_copy(src, dst, sem, block):
    return pltpu.make_async_copy(src.at[block], dst.at[block], sem.at[block])


def degree_body(adj, deg, buf, sem):
    blocks = adj.shape[0]
    for b in range(blocks):
        block_copy(adj, buf, sem, b).start()

    @pl.loop(0, blocks)
    def _(b):
        block_copy(adj, buf, sem, b).wait()
        by_column = jnp.sum(buf[b].astype(F32), axis=1)
        deg[b] = lax.dot_general(
            jnp.ones((8, by_column.shape[1]), F32),
            by_column,
            (((1,), (1,)), ((), ())),
            precision=lax.Precision.HIGHEST,
            preferred_element_type=F32,
        )


def degree_part(adj):
    blocks, rows, _, _ = adj.shape
    return pl.pallas_call(
        degree_body,
        in_specs=[ANY],
        out_specs=VMEM,
        out_shape=jax.ShapeDtypeStruct((blocks, 8, rows), F32),
        scratch_shapes=[pltpu.VMEM(adj.shape, BF16), pltpu.SemaphoreType.DMA((blocks,))],
        compiler_params=PARAMS,
    )(adj)


def split_slots(tiles, adj_block):
    rows = adj_block.shape[0]
    for g in range(rows // 16):
        tiles[:, pl.ds(g * 16, 16), :] = jnp.swapaxes(adj_block[pl.ds(g * 16, 16)], 0, 1)


def backward_body(src, adj, grads, w_neigh, deg, table_out, table, buf, tiles, sem, out_sem):
    blocks, rows, slots, _ = adj.shape
    for b in range(blocks):
        block_copy(adj, buf, sem, b).start()

    @pl.loop(0, table.shape[0], unroll=8)
    def _(c):
        table[c] = jnp.zeros(table.shape[1:], F32)

    @pl.loop(0, blocks)
    def _(b):
        block_copy(adj, buf, sem, b).wait()
        split_slots(tiles, buf.at[b])
        grad_t = lax.dot_general(
            w_neigh[...],
            grads[pl.ds(pl.multiple_of(b * rows, rows), rows), :],
            (((1,), (1,)), ((), ())),
            preferred_element_type=F32,
        )
        grad_t = grad_t / jnp.maximum(deg[b][0:1], 1.0)
        high = grad_t.astype(BF16)
        low = (grad_t - high.astype(F32)).astype(BF16)
        both = jnp.concatenate([high, low], axis=1)
        for k in range(0, slots, 2):
            pair = jnp.concatenate([tiles[k], tiles[k + 1]], axis=1)
            part = jnp.dot(both, jnp.concatenate([pair, pair], axis=0), preferred_element_type=F32)
            table[src[b, k]] += part[:, : part.shape[1] // 2]
            table[src[b, k + 1]] += part[:, part.shape[1] // 2 :]

    @pl.loop(0, table.shape[0], unroll=4)
    def _(c):
        table[c] = table[c].T

    copy = pltpu.make_async_copy(table, table_out, out_sem)
    copy.start()
    copy.wait()


def backward(src, adj, grads, w_neigh, deg, table_blocks):
    blocks, rows, slots, cols = adj.shape
    feat = grads.shape[1]
    return pl.pallas_call(
        backward_body,
        in_specs=[SMEM, ANY, VMEM, VMEM, VMEM],
        out_specs=ANY,
        out_shape=jax.ShapeDtypeStruct((table_blocks, cols, feat), F32),
        scratch_shapes=[
            pltpu.VMEM((table_blocks, feat, cols), F32),
            pltpu.VMEM(adj.shape, BF16),
            pltpu.VMEM((slots, rows, cols), BF16),
            pltpu.SemaphoreType.DMA((blocks,)),
            pltpu.SemaphoreType.DMA,
        ],
        compiler_params=PARAMS,
    )(src, adj, grads, w_neigh, deg)


def forward_body(src, adj, own, hub, halo, num, table, buf, tiles, sem, table_sem):
    blocks, rows, slots, _ = adj.shape
    copies = []
    start = 0
    for i, part in enumerate((own, hub, halo)):
        count = part.shape[0]
        copies.append(pltpu.make_async_copy(part, table.at[pl.ds(start, count)], table_sem.at[i]))
        start += count
    for copy in copies:
        copy.start()
    for b in range(blocks):
        block_copy(adj, buf, sem, b).start()
    for copy in copies:
        copy.wait()

    @pl.loop(0, blocks)
    def _(b):
        block_copy(adj, buf, sem, b).wait()
        split_slots(tiles, buf.at[b])
        total = jnp.zeros((rows, num.shape[1]), F32)
        for k in range(0, slots, 2):
            pair = jnp.concatenate([tiles[k], tiles[k + 1]], axis=1)
            rhs = jnp.concatenate([table[src[b, k]], table[src[b, k + 1]]], axis=0)
            total = total + jnp.dot(pair, rhs, preferred_element_type=F32)
        num[pl.ds(pl.multiple_of(b * rows, rows), rows), :] = total


def forward(src, adj, own, hub, halo):
    blocks, rows, slots, cols = adj.shape
    table_blocks = own.shape[0] + hub.shape[0] + halo.shape[0]
    feat = own.shape[2]
    return pl.pallas_call(
        forward_body,
        in_specs=[SMEM, ANY, ANY, ANY, ANY],
        out_specs=VMEM,
        out_shape=jax.ShapeDtypeStruct((blocks * rows, feat), F32),
        scratch_shapes=[
            pltpu.VMEM((table_blocks, cols, feat), BF16),
            pltpu.VMEM(adj.shape, BF16),
            pltpu.VMEM((slots, rows, cols), BF16),
            pltpu.SemaphoreType.DMA((blocks,)),
            pltpu.SemaphoreType.DMA((3,)),
        ],
        compiler_params=PARAMS,
    )(src, adj, own, hub, halo)


def local(
    features,
    adjacency,
    tile_source,
    hub_rows,
    send_rows,
    send_live,
    target_block,
    w_self,
    w_neigh,
    out_bias,
    out_grad,
):
    highest = lax.Precision.HIGHEST
    own_count, feat = features.shape
    peers = lax.axis_size("dom")
    shares = lax.axis_size("esplit")
    share = lax.axis_index("esplit")
    adj = adjacency[0, 0]
    src = tile_source[0, 0]
    blocks, rows, _, cols = adj.shape
    targets = blocks * rows
    quarter = targets // shares
    hub_idx = hub_rows[0]
    hubs = hub_idx.shape[0]
    lists = send_rows[0]
    slots = lists.shape[1]
    live = jnp.arange(slots, dtype=jnp.int32)[None, :] < send_live[0][:, None]

    hub_local = features[hub_idx]
    halo_send = jnp.where(live[:, :, None], features[lists], jnp.zeros((), features.dtype))
    hub_all = lax.all_gather(hub_local, "dom", axis=0, tiled=True)
    halo_all = lax.all_to_all(halo_send, "dom", split_axis=0, concat_axis=0, tiled=True)

    deg = lax.psum(degree_part(adj)[:, :1], "esplit")
    table_blocks = (own_count + peers * (hubs + slots)) // cols
    deg_rows = jnp.broadcast_to(deg, (blocks, 8, rows))
    table_grad = backward(src, adj, out_grad, w_neigh, deg_rows, table_blocks).reshape(-1, feat)
    own_grad = table_grad[:own_count]
    hub_grad = table_grad[own_count : own_count + peers * hubs].reshape(peers, hubs, feat)
    halo_grad = table_grad[own_count + peers * hubs :].reshape(peers, slots, feat)
    packet = jnp.concatenate([hub_grad, halo_grad], axis=1)
    returned = lax.all_to_all(packet, "dom", split_axis=0, concat_axis=0, tiled=True)

    numerator = forward(
        src,
        adj,
        features.reshape(-1, cols, feat),
        hub_all.reshape(-1, cols, feat),
        halo_all.reshape(-1, cols, feat),
    )
    num = lax.psum_scatter(numerator, "esplit", scatter_dimension=0, tiled=True)

    start_row = target_block[0] * rows
    first = share * quarter
    self_start = start_row + first
    self_rows = lax.dynamic_slice_in_dim(features, self_start, quarter, 0)
    grads = lax.dynamic_slice_in_dim(out_grad, first, quarter, 0)
    grads_wide = grads.astype(F32)
    divisor = jnp.maximum(lax.dynamic_slice_in_dim(deg.reshape(targets), first, quarter, 0), 1.0)
    aggregate = num / divisor[:, None]
    layer_out = (
        jnp.dot(aggregate, w_neigh.astype(F32), precision=highest)
        + jnp.dot(self_rows, w_self, preferred_element_type=F32)
        + out_bias.astype(F32)
    ).astype(BF16)
    contract = (((0,), (0,)), ((), ()))
    weight_grads = jnp.concatenate(
        [
            lax.dot_general(self_rows, grads, contract, preferred_element_type=F32),
            lax.dot_general(aggregate, grads_wide, contract, precision=highest),
            jnp.broadcast_to(jnp.sum(grads_wide, axis=0)[None, :], (8, feat)),
        ],
        axis=0,
    )
    weight_grads = lax.psum(weight_grads, ("dom", "esplit")) / math.sqrt(targets * peers)

    self_grad = lax.dynamic_slice_in_dim(own_grad, self_start, quarter, 0) + jnp.dot(
        grads, w_self.T, preferred_element_type=F32
    )
    own_grad = lax.dynamic_update_slice_in_dim(own_grad, self_grad, self_start, 0)
    own_grad = own_grad.at[hub_idx].add(jnp.sum(returned[:, :hubs], axis=0))
    own_grad = own_grad.at[lists].add(jnp.where(live[:, :, None], returned[:, hubs:], 0.0))
    grad_features = lax.psum_scatter(own_grad, "esplit", scatter_dimension=0, tiled=True)
    return (
        layer_out,
        grad_features,
        weight_grads[:feat],
        weight_grads[feat : 2 * feat],
        weight_grads[2 * feat],
    )


def solution(mesh):
    in_specs = (
        P("dom", None),
        P("dom", "esplit", None, None, None, None),
        P("dom", "esplit", None, None),
        P("dom", None),
        P("dom", None, None),
        P("dom", None),
        P("dom"),
        P(),
        P(),
        P(),
        P("dom", None),
    )
    out_specs = (P(("dom", "esplit"), None), P(("dom", "esplit"), None), P(), P(), P())
    return jax.shard_map(local, mesh=mesh, in_specs=in_specs, out_specs=out_specs, check_vma=False)
```

time: 653 us -> 523 us (0.80)
  other arithmetic: 233 us -> 55.1 us
  waiting for transfers between devices: 154 us -> 325 us
  blocking collectives: 76.8 us -> 11.9 us
  local copies, waits for them, and re-layouts: 97.6 us -> 33.7 us
  Pallas kernels: 0 us -> 59.8 us
  matrix products: 54 us -> 6.5 us
    all_gather x0 -> x1, waiting for transfers between devices: none -> 123 us  [local(): hub_all = lax.all_gather(hub_local, 'dom', axis=0, tiled=True)]
    scatter-add x3 -> x2, other arithmetic: 140 us -> 36.3 us  [the longest x1 26.7 us: local(): own_grad.at[lists].add(jnp.where(live[:, :, None], returned[:, hubs:], 0.0))]
    psum x2 -> x1, blocking collectives: 76.8 us -> 11.9 us  [local(): deg = lax.psum(degree_part(adj)[:, :1], 'esplit')]
    pallas_call x0 -> x3, Pallas kernels: none -> 59.8 us  [the longest x1 29.9 us: backward(): pl.pallas_call(backward_body, in_specs=[SMEM, ANY, VMEM, VMEM, VMEM], out...]
    concatenate x3 -> x2, other arithmetic: 65.9 us -> 8.99 us  [the longest x1 8.34 us: local(): packet = jnp.concatenate([hub_grad, halo_grad], axis=1)]
    dot_general x8 -> x5, matrix products: 54 us -> 6.5 us  [the longest x1 1.84 us: local(): jnp.dot(grads, w_self.T, preferred_element_type=F32)]
    dot_general x1 -> x0, local copies, waits for them, and re-layouts: 33.4 us -> none  [local(): jnp.einsum('bikj,bif->bkjf', tile_vals.astype(jnp.float32), numer_grad.re...]
    psum x2 -> x1, waiting for transfers between devices: 74.4 us -> 102 us  [local(): lax.psum(weight_grads, ('dom', 'esplit')) / math.sqrt(targets * peers)]
  transfers between devices with their start and end apart: 5 -> 6, of which waited for: 3 -> 4; matrix products, arithmetic and copies ran while one was open for 56% -> 14% of each run, Pallas kernels for 0% -> 11%
where the time goes in v1:
time: 523 us; the launch traced here: 522 us
  waiting for transfers between devices  325 us (62%)
  Pallas kernels  59.8 us (11%)
  other arithmetic  55.1 us (11%)
  local copies, waits for them, and re-layouts  33.7 us (6%)
  starting transfers between devices  15.1 us (3%)
  between operations  14.6 us (3%)
  blocking collectives  11.9 us (2%)
  matrix products  6.5 us (1%)
    all_gather x1, waiting for transfers between devices, local(): hub_all = lax.all_gather(hub_local, 'dom', axis=0, tiled=True)  123 us
    psum x1, waiting for transfers between devices, local(): lax.psum(weight_grads, ('dom', 'esplit')) / math.sqrt(targets * peers)  102 us
    reduce_scatter x1, waiting for transfers between devices, local(): lax.psum_scatter(own_grad, 'esplit', scatter_dimension=0, tiled=True)  78.8 us
    pallas_call x1, Pallas kernels, backward(): pl.pallas_call(backward_body, in_specs=[SMEM, ANY, VMEM, VMEM, VMEM], out...  29.9 us
    scatter-add x1, other arithmetic, local(): own_grad.at[lists].add(jnp.where(live[:, :, None], returned[:, hubs:], 0.0))  26.7 us
    reduce_scatter x1, waiting for transfers between devices, local(): num = lax.psum_scatter(numerator, 'esplit', scatter_dimension=0, tiled=True)  21 us
    pallas_call x1, Pallas kernels, forward(): pl.pallas_call(forward_body, in_specs=[SMEM, ANY, ANY, ANY, ANY], out_spe...  20.9 us
    gather x1, local copies, waits for them, and re-layouts, local(): features[lists]  13.8 us
  transfers between devices with their start and end apart: 6, of which 4 were waited for; matrix products, arithmetic and copies ran while one was open for 14% of the time, Pallas kernels for 11%

profile of v1, /device:TPU:0, one launch (start us, length us, event | category | flops | bytes accessed | tf_op | source)
XLA Modules:
  0.0 521.7 jit_solution(12364703714225699633)
XLA Ops:
  7.2 0.0 copy-start
  7.2 0.7 iota_compare_fusion
  7.9 0.7 broadcast_clamp_fusion
  8.6 13.8 %gather_fusion.1 = bf16[4096,128]{1,0:T(8,128)(2,1)S(1)} fusion(bf16[16384,128]{1,0:T(8,128)(2,1)} %param.11, s32[4096]{0:T(1024)S(1)} %broadcast_clamp_fusion), kind=kCustom, calls=%fused_computation.1 | custom fusion | bytes 2113536 | tf_op jit(solution)/shard_map/gather | solution.py:193
  22.4 1.5 broadcast_select_fusion
  23.9 7.4 %all-to-all-start = ((bf16[32,128,128]{2,1,0:T(8,128)(2,1)}), bf16[32,128,128]{2,1,0:T(8,128)(2,1)S(1)}, u32[]{:S(2)}, u32[]{:S(2)}) async-start(bf16[32,128,128]{2,1,0:T(8,128)(2,1)} %broadcast_select_fusion), calls=%async_computation | async-start | bytes 2097152 | tf_op jit(solution)/shard_map/all_to_all | solution.py:195
  31.3 8.9 %shard_map.147 = f32[16,8,128]{2,1,0:T(8,128)} custom-call(bf16[16,128,32,128]{3,2,1,0:T(8,128)(2,1)} %bitcast.29), custom_call_target="tpu_custom_call" | custom-call | tf_op jit(solution)/shard_map/pallas_call | solution.py:43
  40.2 0.8 slice.46
  41.1 11.9 %psum.14 = f32[16,1,128]{2,1,0:T(1,128)S(1)} all-reduce(f32[16,1,128]{2,1,0:T(1,128)S(1)} %slice.46), channel_id=1, replica_groups=mesh['dom'=32,'esplit'=4] {'esplit'}, use_global_device_ids=true, to_apply=%region_1.2 | all-reduce | flops 2048 | bytes 16384 | tf_op jit(solution)/shard_map/psum | solution.py:197
  52.9 0.6 broadcast_in_dim.31.deg
  53.6 29.9 %shard_map.148 = f32[288,128,128]{2,1,0:T(8,128)} custom-call(s32[16,32]{1,0:T(8,128)} %bitcast.39, bf16[16,128,32,128]{3,2,1,0:T(8,128)(2,1)} %bitcast.30, bf16[2048,128]{1,0:T(8,128)(2,1)} %grads.1, bf16[128,128]{1,0:T(8,128)(2,1)} %w_neigh.1, f32[16,8,128]{2,1,0:T(8,128)} %broadcast_in_dim.31.deg), custom_call_target="tpu_custom_call" | custom-call | tf_op jit(solution)/shard_map/pallas_call | solution.py:100
  83.5 0.0 slice-start
  83.5 11.0 %fusion.16 = (f32[128,128,128]{2,1,0:T(8,128)}, f32[128,128,128]{2,1,0:T(8,128)}) fusion(f32[288,128,128]{2,1,0:T(8,128)} %shard_map.148), kind=kLoop, calls=%fused_computation.37 | loop fusion | bytes 33554432 | tf_op jit(solution)/shard_map/slice | solution.py:202
  94.5 0.0 slice-done
  94.5 8.3 %pad_maximum_fusion = f32[32,640,128]{2,1,0:T(8,128)} fusion(f32[32,128,128]{2,1,0:T(8,128)S(1)} %slice-done, f32[32,512,128]{2,1,0:T(8,128)} %bitcast.33), kind=kLoop, calls=%fused_computation.4 | loop fusion | flops 2621440 | bytes 20971520 | tf_op jit(solution)/shard_map/concatenate | solution.py:204
  102.8 0.0 copy-start.5
  102.9 0.0 all-to-all-done.halo
  102.9 0.0 copy-start.1
  102.9 1.0 copy-done.1
  103.8 7.5 %all-to-all-start.1 = ((f32[32,640,128]{2,1,0:T(8,128)}), f32[32,640,128]{2,1,0:T(8,128)}, u32[]{:S(2)}, u32[]{:S(2)}) async-start(f32[32,640,128]{2,1,0:T(8,128)} %pad_maximum_fusion), calls=%async_computation.2 | async-start | bytes 20971520 | tf_op jit(solution)/shard_map/all_to_all | solution.py:205
  111.3 0.0 all-gather.3.cloned.1.call-start
  111.4 0.0 copy-done.5
  111.4 4.4 gather_fusion
  115.8 0.0 all-gather.3.cloned.1.call-update
  115.8 0.0 reduce-scatter.3.cloned.1.call-start
  115.9 123.3 %all-gather.3.cloned.1.call-done = bf16[16384,128]{1,0:T(8,128)(2,1)} async-done(((bf16[512,128]{1,0:T(8,128)(2,1)}), bf16[16384,128]{1,0:T(8,128)(2,1)}) %all-gather.3.cloned.1.call-update) | async-done | bytes 4194320 | tf_op jit(solution)/shard_map/all_gather | solution.py:194
  239.2 0.0 copy-start.2
  239.2 0.0 copy-start.3
  239.2 20.9 %shard_map.146 = f32[2048,128]{1,0:T(8,128)} custom-call(s32[16,32]{1,0:T(8,128)} %bitcast.40, bf16[16,128,32,128]{3,2,1,0:T(8,128)(2,1)} %bitcast.31, bf16[128,128,128]{2,1,0:T(8,128)(2,1)} %bitcast.32, bf16[128,128,128]{2,1,0:T(8,128)(2,1)} %bitcast.35, bf16[32,128,128]{2,1,0:T(8,128)(2,1)} %copy-done.1), custom_call_target="tpu_custom_call" | custom-call | tf_op jit(solution)/shard_map/pallas_call | solution.py:147
  260.1 0.0 reduce-scatter.3.cloned.1.call-update
  260.2 0.0 all-reduce.2.cloned.1.call-start
  260.9 0.0 copy-done.2
  260.9 0.1 convert_reduce_fusion
  261.0 0.1 dynamic-slice_maximum_fusion
  261.0 1.1 fusion.3
  262.2 0.0 copy-done.3
  262.2 0.0 copy-done
  262.2 1.8 fusion
  264.0 0.0 all-to-all-done.1
  264.0 3.8 slice_reduce_fusion
  267.8 21.0 %reduce-scatter.3.cloned.1.call-done = f32[512,128]{1,0:T(8,128)} async-done(((f32[2048,128]{1,0:T(8,128)}), f32[512,128]{1,0:T(8,128)}) %reduce-scatter.3.cloned.1.call-update) | async-done | bytes 262160 | tf_op jit(solution)/shard_map/reduce_scatter | solution.py:214
  288.9 1.5 fusion.6
  290.4 0.7 pad_maximum_fusion.1
  291.0 0.0 all-reduce.2.cloned.1.call-update
  291.0 0.0 reduce-scatter.5.cloned.1.call-start
  291.1 2.0 slice_select_fusion
  293.1 9.6 %scatter_fusion = f32[16384,128]{1,0:T(8,128)} fusion(f32[16384,128]{1,0:T(8,128)} %fusion, s32[512]{0:T(512)S(1)} %bitcast.42, f32[512,128]{1,0:T(8,128)S(1)} %slice_reduce_fusion), kind=kCustom, calls=%fused_computation.2 | custom fusion | flops 65536 | bytes 788480 | tf_op jit(solution)/shard_map/scatter-add | solution.py:244
  302.6 26.7 %scatter_fusion.1 = f32[16384,128]{1,0:T(8,128)} fusion(f32[16384,128]{1,0:T(8,128)} %scatter_fusion, s32[4096]{0:T(1024)S(1)} %fusion.11, f32[4096,128]{1,0:T(8,128)S(1)} %bitcast.34), kind=kCustom, calls=%fused_computation.3 | custom fusion | flops 524288 | bytes 6307840 | tf_op jit(solution)/shard_map/scatter-add | solution.py:245
  329.3 0.0 copy-start.7
  329.3 0.0 copy-start.4
  329.3 0.0 copy-start.6
  329.3 0.0 reduce-scatter.5.cloned.1.call-update
  329.4 0.6 copy-done.7
  330.0 0.1 copy-done.4
  330.1 0.2 copy-done.6
  330.3 0.3 fusion.10
  330.7 1.7 fusion.2
  332.4 101.8 %all-reduce.2.cloned.1.call-done = f32[264,128]{1,0:T(8,128)} async-done(((f32[264,128]{1,0:T(8,128)}), f32[264,128]{1,0:T(8,128)}) %all-reduce.2.cloned.1.call-update) | async-done | bytes 135184 | tf_op jit(solution)/shard_map/psum | solution.py:238
  434.2 0.9 broadcast_multiply_fusion
  435.1 0.5 slice_bitcast_fusion
  435.6 0.7 fusion.17
  436.3 78.8 %reduce-scatter.5.cloned.1.call-done = f32[4096,128]{1,0:T(8,128)} async-done(((f32[16384,128]{1,0:T(8,128)}), f32[4096,128]{1,0:T(8,128)}) %reduce-scatter.5.cloned.1.call-update) | async-done | bytes 2097168 | tf_op jit(solution)/shard_map/reduce_scatter | solution.py:246
  (5 shorter events, 0.0 us)
Async XLA Ops:
  7.2 255.0 %copy-start = (bf16[128,128]{1,0:T(8,128)(2,1)S(1)}, bf16[128,128]{1,0:T(8,128)(2,1)}, u32[]{:S(2)}) copy-start(bf16[128,128]{1,0:T(8,128)(2,1)} %param.18) | copy-start | bytes 98308
  23.9 78.9 %all-to-all-start = ((bf16[32,128,128]{2,1,0:T(8,128)(2,1)}), bf16[32,128,128]{2,1,0:T(8,128)(2,1)S(1)}, u32[]{:S(2)}, u32[]{:S(2)}) async-start(bf16[32,128,128]{2,1,0:T(8,128)(2,1)} %broadcast_select_fusion), calls=%async_computation | async-start | bytes 2097152 | tf_op jit(solution)/shard_map/all_to_all | solution.py:195
  83.5 11.0 %slice-start = ((f32[288,128,128]{2,1,0:T(8,128)}), f32[32,128,128]{2,1,0:T(8,128)S(1)}, s32[]{:S(2)}) async-start(f32[288,128,128]{2,1,0:T(8,128)} %shard_map.148), calls=%async_computation.8 | async-start | bytes 4194304 | tf_op jit(solution)/shard_map/slice | solution.py:203
  102.8 8.5 %copy-start.5 = (s32[1,512]{1,0:T(1,128)S(1)}, s32[1,512]{1,0:T(1,128)}, u32[]{:S(2)}) copy-start(s32[1,512]{1,0:T(1,128)} %param.14) | copy-start | bytes 6148
  102.9 1.0 copy-start.1
  103.8 160.2 %all-to-all-start.1 = ((f32[32,640,128]{2,1,0:T(8,128)}), f32[32,640,128]{2,1,0:T(8,128)}, u32[]{:S(2)}, u32[]{:S(2)}) async-start(f32[32,640,128]{2,1,0:T(8,128)} %pad_maximum_fusion), calls=%async_computation.2 | async-start | bytes 20971520 | tf_op jit(solution)/shard_map/all_to_all | solution.py:205
  111.3 127.9 %all-gather.3.cloned.1.call-start = ((), (), s32[]{:S(2)}) async-start(), calls=%async_computation.7 | async-start | bytes 4325376 | tf_op jit(solution)/shard_map/all_gather | solution.py:194
  115.8 173.1 %reduce-scatter.3.cloned.1.call-start = ((), (), s32[]{:S(2)}) async-start(), calls=%async_computation.4 | async-start | bytes 1310720 | tf_op jit(solution)/shard_map/reduce_scatter | solution.py:214
  239.2 21.7 %copy-start.2 = (bf16[2048,128]{1,0:T(8,128)(2,1)S(1)}, bf16[2048,128]{1,0:T(8,128)(2,1)}, u32[]{:S(2)}) copy-start(bf16[2048,128]{1,0:T(8,128)(2,1)} %grads.1) | copy-start | bytes 1572868
  239.2 23.0 %copy-start.3 = (s32[1,32,128]{2,1,0:T(8,128)S(1)}, s32[1,32,128]{2,1,0:T(8,128)}, u32[]{:S(2)}) copy-start(s32[1,32,128]{2,1,0:T(8,128)} %param.15) | copy-start | bytes 49156
  260.2 174.0 %all-reduce.2.cloned.1.call-start = ((), (), s32[]{:S(2)}) async-start(), calls=%async_computation.6 | async-start | bytes 270336 | tf_op jit(solution)/shard_map/psum | solution.py:238
  291.0 224.1 %reduce-scatter.5.cloned.1.call-start = ((), (), s32[]{:S(2)}) async-start(), calls=%async_computation.5 | async-start | bytes 10485760 | tf_op jit(solution)/shard_map/reduce_scatter | solution.py:246
  329.3 0.7 copy-start.7
  329.3 0.8 copy-start.4
  329.3 1.0 copy-start.6
Sparse Core Ops, SparseCore 0:
  116.0 123.1 all-gather.2
  260.3 28.5 reduce-scatter.2
  294.4 139.7 all-reduce.1
  437.1 77.9 reduce-scatter.4

commit v2 on v1

v2 whole, which is shorter than its diff:
```python
import math

import jax
import jax.numpy as jnp
from jax import lax
from jax.experimental import pallas as pl
from jax.experimental.pallas import tpu as pltpu
from jax.sharding import PartitionSpec as P

F32 = jnp.float32
BF16 = jnp.bfloat16
I16 = jnp.int16
I32 = jnp.int32
MESH = pl.DeviceIdType.MESH
DMA = pltpu.SemaphoreType.DMA
VMEM_LIMIT = 56 * 2**20
ANY = pl.BlockSpec(memory_space=pl.ANY)
SMEM = pl.BlockSpec(memory_space=pltpu.SMEM)
VMEM = pl.BlockSpec(memory_space=pltpu.VMEM)
PARAMS = pltpu.CompilerParams(vmem_limit_bytes=VMEM_LIMIT)
BLK = 128
TOP = 32767.0


def remote_params(number):
    return pltpu.CompilerParams(
        vmem_limit_bytes=VMEM_LIMIT, collective_id=number, has_side_effects=True
    )


class Place:
    def __init__(self):
        self.d = lax.axis_index("dom")
        self.z = lax.axis_index("esplit")
        self.core = lax.rem(self.d, 2)
        self.x = lax.rem(lax.div(self.d, 2), 4)
        self.y = lax.div(self.d, 8)

    def at(self, axis):
        return {"x": self.x, "y": self.y, "z": self.z}[axis]

    def step(self, axis, by):
        return lax.rem(self.at(axis) + (by + 4), 4)

    def device(self, axis, by):
        if axis == "core":
            return (self.d + 1 - 2 * self.core, self.z)
        there = self.step(axis, by)
        if axis == "z":
            return (self.d, there)
        if axis == "x":
            return ((self.y * 4 + there) * 2 + self.core, self.z)
        return ((there * 4 + self.x) * 2 + self.core, self.z)

    def share(self):
        return lax.rem(self.z - self.d + 32, 4)


class Links:
    def __init__(self, send_sem, recv_sem):
        self.send_sem, self.recv_sem, self.used, self.made = send_sem, recv_sem, 0, []

    def send(self, src, dst, device):
        copy = pltpu.make_async_remote_copy(
            src_ref=src,
            dst_ref=dst,
            send_sem=self.send_sem.at[self.used],
            recv_sem=self.recv_sem.at[self.used],
            device_id=device,
            device_id_type=MESH,
        )
        self.used += 1
        copy.start()
        self.made.append(copy)
        return copy

    def drain(self):
        for copy in self.made:
            copy.wait_send()


def greet(place, near, far=False):
    barrier = pltpu.get_barrier_semaphore()
    for axis, by in near:
        pl.semaphore_signal(
            barrier, inc=1, device_id=place.device(axis, by), device_id_type=MESH
        )
    count = len(near)
    if far:
        share = place.share()
        for j in range(8):
            peer = j * 4 + share

            @pl.when(peer != place.d)
            def _():
                pl.semaphore_signal(
                    barrier, inc=1, device_id=(peer, place.z), device_id_type=MESH
                )

        mine = (lax.rem(place.d, 4) == share).astype(I32)
        pl.semaphore_wait(barrier, count + 8 - mine)
    else:
        pl.semaphore_wait(barrier, count)


def peer_copy(place, src, dst, j, send_sem, recv_sem, out):
    return pltpu.make_async_remote_copy(
        src_ref=src,
        dst_ref=dst,
        send_sem=send_sem.at[j],
        recv_sem=recv_sem.at[lax.div(place.d, 4) if out else j],
        device_id=(j * 4 + place.share(), place.z),
        device_id_type=MESH,
    )


def block_copy(src, dst, sem, block):
    return pltpu.make_async_copy(src.at[block], dst.at[block], sem.at[block])


def exchange_body(
    adj, hub_in, halo_in, deg_out, hub_out, halo_out,
    buf, deg_all, deg_mine, adj_sem, local_sem, send_sem, recv_sem, far_send, far_recv,
):
    place = Place()
    x, y, c, d, z = place.x, place.y, place.core, place.d, place.z
    share = place.share()
    blocks = adj.shape[0]
    for b in range(blocks):
        block_copy(adj, buf, adj_sem, b).start()
    own_hub = pltpu.make_async_copy(hub_in, hub_out.at[y, x, c], local_sem.at[0])
    own_hub.start()
    near = [("x", 1), ("x", -1), ("y", 1), ("y", -1), ("z", 1), ("z", -1), ("z", 2), ("core", 1)]
    greet(place, near, far=True)
    links = Links(send_sem, recv_sem)

    first = {}
    for axis, half in (("x", 0), ("y", 1)):
        for by in (1, -1):
            first[axis, by] = links.send(
                hub_in.at[half], hub_out.at[y, x, c, half], place.device(axis, by)
            )
    here = lax.div(d, 4)
    for j in range(8):

        @pl.when(j * 4 + share != d)
        def _():
            there = halo_out.at[here, lax.rem(d, 4)]
            peer_copy(place, halo_in.at[j], there, j, far_send, far_recv, True).start()

        @pl.when(j * 4 + share == d)
        def _():
            keep = pltpu.make_async_copy(halo_in.at[j], halo_out.at[j, share], local_sem.at[1])
            keep.start()
            keep.wait()

    def degrees(low, high):
        @pl.loop(low, high)
        def _(b):
            block_copy(adj, buf, adj_sem, b).wait()
            by_column = jnp.sum(buf[b].astype(F32), axis=1)
            rows = lax.dot_general(
                jnp.ones((8, by_column.shape[1]), F32),
                by_column,
                (((1,), (1,)), ((), ())),
                precision=lax.Precision.HIGHEST,
                preferred_element_type=F32,
            )
            deg_mine[pl.ds(b, 1), :] = rows[0:1]

    degrees(0, 4)
    relay = {}
    for axis, half in (("x", 0), ("y", 1)):
        for by, part in ((1, 0), (-1, 1)):
            first[axis, by].wait_recv()
            back = place.step(axis, -by)
            at = (y, back) if axis == "x" else (back, x)
            piece = hub_out.at[at[0], at[1], c, half, pl.ds(part * 128, 128)]
            relay[axis, by] = links.send(piece, piece, place.device(axis, by))
    degrees(4, blocks)
    deg_all[z] = deg_mine[...]
    deg_copies = [
        links.send(deg_mine, deg_all.at[z], place.device("z", by)) for by in (1, -1, 2)
    ]

    own_hub.wait()
    second = {}
    for axis, other, half in (("x", "y", 0), ("y", "x", 1)):
        relay[axis, 1].wait_recv()
        relay[axis, -1].wait_recv()
        line = hub_out.at[y, :, c, half] if axis == "x" else hub_out.at[:, x, c, half]
        for by in (1, -1):
            second[other, by] = links.send(line, line, place.device(other, by))
    for axis, half in (("x", 0), ("y", 1)):
        line = hub_out.at[y, :, c, half] if axis == "x" else hub_out.at[:, x, c, half]
        second["core", axis] = links.send(line, line, place.device("core", 1))

    for j in range(8):

        @pl.when(j * 4 + share != d)
        def _():
            come = peer_copy(
                place, halo_in.at[j], halo_out.at[j, share], j, far_send, far_recv, False
            )
            come.wait_recv()
            come.wait_send()

    mine = halo_out.at[:, share]
    halo_first = {by: links.send(mine, mine, place.device("z", by)) for by in (1, -1)}

    third = {}
    last = []
    for axis, other, half in (("x", "y", 0), ("y", "x", 1)):
        for by, part in ((1, 0), (-1, 1)):
            second[other, by].wait_recv()
            back = place.step(other, -by)
            if axis == "x":
                line = hub_out.at[back, :, c, half]
                piece = hub_out.at[back, pl.ds(part * 2, 2), c, half]
            else:
                line = hub_out.at[:, back, c, half]
                piece = hub_out.at[pl.ds(part * 2, 2), back, c, half]
            third[other, by] = links.send(piece, piece, place.device(other, by))
            last.append(links.send(line, line, place.device("core", 1)))

    halo_relay = []
    for by, part in ((1, 0), (-1, 1)):
        halo_first[by].wait_recv()
        back = lax.rem(place.step("z", -by) - d + 32, 4)
        piece = halo_out.at[pl.ds(part * 4, 4), back]
        halo_relay.append(links.send(piece, piece, place.device("z", by)))

    for axis, other, half in (("x", "y", 0), ("y", "x", 1)):
        third[other, 1].wait_recv()
        third[other, -1].wait_recv()
        back = place.step(other, 2)
        line = hub_out.at[back, :, c, half] if axis == "x" else hub_out.at[:, back, c, half]
        last.append(links.send(line, line, place.device("core", 1)))

    for copy in deg_copies:
        copy.wait_recv()
    deg_out[...] = (deg_all[0] + deg_all[1]) + (deg_all[2] + deg_all[3])
    for copy in halo_relay + last + [second["core", "x"], second["core", "y"]]:
        copy.wait_recv()
    links.drain()


def exchange(adj, hub_in, halo_in):
    blocks, rows, _, _ = adj.shape
    hubs, feat = hub_in.shape
    return pl.pallas_call(
        exchange_body,
        in_specs=[ANY, ANY, ANY],
        out_specs=[VMEM, ANY, ANY],
        out_shape=[
            jax.ShapeDtypeStruct((blocks, rows), F32),
            jax.ShapeDtypeStruct((4, 4, 2, 2, hubs // 2, feat), BF16),
            jax.ShapeDtypeStruct((8, 4) + halo_in.shape[1:], BF16),
        ],
        scratch_shapes=[
            pltpu.VMEM(adj.shape, BF16),
            pltpu.VMEM((4, blocks, rows), F32),
            pltpu.VMEM((blocks, rows), F32),
            DMA((blocks,)),
            DMA((2,)),
            DMA((32,)),
            DMA((32,)),
            DMA((8,)),
            DMA((8,)),
        ],
        compiler_params=remote_params(0),
    )(adj, hub_in.reshape(2, hubs // 2, feat), halo_in)


def split_slots(tiles, adj_block):
    rows = adj_block.shape[0]
    for g in range(rows // 16):
        tiles[:, pl.ds(g * 16, 16), :] = jnp.swapaxes(adj_block[pl.ds(g * 16, 16)], 0, 1)


def products_body(
    src, adj, grads, w_neigh, deg, own, hub, halo, own_out, far_out, num,
    table, rows_in, buf, tiles, sem, in_sem, out_sem,
):
    blocks, rows, slots, _ = adj.shape
    for b in range(blocks):
        block_copy(adj, buf, sem, b).start()
    copies = []
    start = 0
    for i, part in enumerate((own, hub, halo)):
        count = part.shape[0]
        copies.append(pltpu.make_async_copy(part, rows_in.at[pl.ds(start, count)], in_sem.at[i]))
        start += count
    for copy in copies:
        copy.start()

    @pl.loop(0, table.shape[0], unroll=8)
    def _(c):
        table[c] = jnp.zeros(table.shape[1:], F32)

    for copy in copies:
        copy.wait()

    @pl.loop(0, blocks)
    def _(b):
        block_copy(adj, buf, sem, b).wait()
        split_slots(tiles, buf.at[b])
        grad_t = lax.dot_general(
            w_neigh[...],
            grads[pl.ds(pl.multiple_of(b * rows, rows), rows), :],
            (((1,), (1,)), ((), ())),
            preferred_element_type=F32,
        )
        grad_t = grad_t / jnp.maximum(deg[pl.ds(b, 1), :], 1.0)
        high = grad_t.astype(BF16)
        low = (grad_t - high.astype(F32)).astype(BF16)
        both = jnp.concatenate([high, low], axis=1)
        total = jnp.zeros((rows, num.shape[1]), F32)
        for k in range(0, slots, 2):
            c0, c1 = src[b, k], src[b, k + 1]
            pair = jnp.concatenate([tiles[k], tiles[k + 1]], axis=1)
            part = jnp.dot(both, jnp.concatenate([pair, pair], axis=0), preferred_element_type=F32)
            table[c0] += part[:, : part.shape[1] // 2]
            table[c1] += part[:, part.shape[1] // 2 :]
            rhs = jnp.concatenate([rows_in[c0], rows_in[c1]], axis=0)
            total = total + jnp.dot(pair, rhs, preferred_element_type=F32)
        num[pl.ds(pl.multiple_of(b * rows, rows), rows), :] = total

    own_blocks = own.shape[0]
    far_blocks = table.shape[0] - own_blocks
    far = pltpu.make_async_copy(table.at[pl.ds(own_blocks, far_blocks)], far_out, out_sem.at[0])
    far.start()
    outs = []
    step = own_blocks // 4
    for g in range(4):

        @pl.loop(g * step, (g + 1) * step, unroll=4)
        def _(c):
            table[c] = table[c].T

        part = pl.ds(g * step, step)
        outs.append(pltpu.make_async_copy(table.at[part], own_out.at[part], out_sem.at[1 + g]))
        outs[-1].start()
    for copy in outs:
        copy.wait()
    far.wait()


def products(src, adj, grads, w_neigh, deg, own, hub, halo):
    blocks, rows, slots, cols = adj.shape
    feat = grads.shape[1]
    far_blocks = hub.shape[0] + halo.shape[0]
    table_blocks = own.shape[0] + far_blocks
    return pl.pallas_call(
        products_body,
        in_specs=[SMEM, ANY, VMEM, VMEM, VMEM, ANY, ANY, ANY],
        out_specs=[ANY, ANY, VMEM],
        out_shape=[
            jax.ShapeDtypeStruct((own.shape[0], cols, feat), F32),
            jax.ShapeDtypeStruct((far_blocks, feat, cols), F32),
            jax.ShapeDtypeStruct((blocks * rows, feat), F32),
        ],
        scratch_shapes=[
            pltpu.VMEM((table_blocks, feat, cols), F32),
            pltpu.VMEM((table_blocks, cols, feat), BF16),
            pltpu.VMEM(adj.shape, BF16),
            pltpu.VMEM((slots, rows, cols), BF16),
            DMA((blocks,)),
            DMA((3,)),
            DMA((5,)),
        ],
        compiler_params=PARAMS,
    )(src, adj, grads, w_neigh, deg, own, hub, halo)


def encode(block):
    top = jnp.maximum(jnp.max(jnp.abs(block), axis=0, keepdims=True), 1e-33)
    return jnp.round(block * (TOP / top)).astype(I32).astype(I16), top * (1.0 / TOP)


def decode(code, scale):
    return code.astype(I32).astype(F32) * scale


class Packet:
    def __init__(self, codes, scales=None):
        self.codes, self.scales = codes, scales

    def put(self, i, block):
        if self.scales is None:
            self.codes[i] = block
        else:
            self.codes[i], self.scales[i] = encode(block)

    def get(self, i):
        if self.scales is None:
            return self.codes[i]
        return decode(self.codes[i], self.scales[i])

    def send(self, links, there, device):
        copies = [links.send(self.codes, there.codes, device)]
        if self.scales is not None:
            copies.append(links.send(self.scales, there.scales, device))
        return copies


class RingSum:
    def __init__(self, place, links, axis, count, load, out_bufs, in_bufs):
        self.place, self.links, self.axis, self.count, self.load = place, links, axis, count, load
        self.out = [Packet(*[ref.at[m] for ref in out_bufs]) for m in range(6)]
        self.come = [Packet(*[ref.at[m] for ref in in_bufs]) for m in range(6)]
        self.copies = {}

    def push(self, m, by, block):
        @pl.loop(0, self.count)
        def _(i):
            self.out[m].put(i, block(i))

        self.copies[m] = self.out[m].send(
            self.links, self.come[m], self.place.device(self.axis, by)
        )

    def wait(self, m):
        for copy in self.copies[m]:
            copy.wait_recv()

    def start(self):
        opposite = self.place.step(self.axis, 2)
        for m, by, half in ((0, 1, 0), (1, -1, 1)):
            self.push(m, by, lambda i, half=half: self.load(opposite, half, i))
        for m, by, half in ((2, 1, 1), (3, -1, 0)):
            there = self.place.step(self.axis, by)
            self.push(m, by, lambda i, there=there, half=half: self.load(there, half, i))

    def relay(self):
        for m, by, half in ((4, 1, 0), (5, -1, 1)):
            there = self.place.step(self.axis, by)
            self.wait(m - 4)
            self.push(
                m,
                by,
                lambda i, there=there, half=half, m=m: self.load(there, half, i)
                + self.come[m - 4].get(i),
            )

    def finish(self, store):
        here = self.place.at(self.axis)
        for half, a, b in ((0, 4, 3), (1, 5, 2)):
            self.wait(a)
            self.wait(b)

            @pl.loop(0, self.count)
            def _(i):
                store(
                    half,
                    i,
                    self.load(here, half, i) + (self.come[a].get(i) + self.come[b].get(i)),
                )


def ring_scratch(count, coded):
    tile = (6, count, BLK, BLK)
    if not coded:
        return [pltpu.VMEM(tile, F32)] * 2
    pair = [pltpu.VMEM(tile, I16), pltpu.VMEM((6, count, 1, BLK), F32)]
    return pair + pair


def ring_bufs(refs, coded):
    n = 2 if coded else 1
    return refs[:n], refs[n:]


def owners_body(far, num_in, hub_out, halo_out, num_out, mine, theirs, lists, num, *rest):
    (core_out, core_scale_out, core_in, core_scale_in), rest = rest[:4], rest[4:]
    rings = []
    for coded in (True, True, True, True, True, False):
        n = 4 if coded else 2
        rings.append(ring_bufs(rest[:n], coded))
        rest = rest[n:]
    line_x, line_y, list_sum, list_out, list_scale_out, list_in, list_scale_in = rest[:7]
    load_sem, send_sem, recv_sem, far_send, far_recv, far_send2, far_recv2 = rest[7:]
    place = Place()
    x, y, c, d, z = place.x, place.y, place.core, place.d, place.z
    share = place.share()
    links = Links(send_sem, recv_sem)

    hub_far = far.at[pl.ds(0, 128)].reshape(16, 2, 4, BLK, BLK)
    loads = [
        pltpu.make_async_copy(far.at[pl.ds(128, 32)], lists, load_sem.at[0]),
        pltpu.make_async_copy(num_in, num, load_sem.at[1]),
    ]
    for g in range(4):
        loads.append(
            pltpu.make_async_copy(
                hub_far.at[pl.ds(g * 4, 4), 1 - c], theirs.at[pl.ds(g * 4, 4)], load_sem.at[2 + g]
            )
        )
    loads.append(pltpu.make_async_copy(hub_far.at[:, c], mine, load_sem.at[6]))
    for load in loads:
        load.start()
    near = [("x", 1), ("x", -1), ("y", 1), ("y", -1), ("z", 1), ("z", -1), ("core", 1)]
    greet(place, near, far=True)

    def ring(which, axis, count, load):
        return RingSum(place, links, axis, count, load, *rings[which])

    def list_for(there, half, i):
        return lists[(half * 4 + i) * 4 + lax.rem(there - d + 32, 4)]

    list_ring = ring(4, "z", 4, list_for)
    num_ring = ring(5, "z", 2, lambda there, half, i: num[there * 4 + half * 2 + i])
    loads[0].wait()
    list_ring.start()
    loads[1].wait()
    num_ring.start()

    core_copies = []
    for g in range(4):
        loads[2 + g].wait()

        @pl.loop(0, 16)
        def _(i):
            code, scale = encode(theirs[g * 4 + lax.div(i, 4), lax.rem(i, 4)])
            core_out[g, i] = code
            core_scale_out[g, i] = scale

        there = place.device("core", 1)
        core_copies.append(
            [
                links.send(core_out.at[g], core_in.at[g], there),
                links.send(core_scale_out.at[g], core_scale_in.at[g], there),
            ]
        )
    list_ring.relay()
    num_ring.relay()
    loads[6].wait()
    for g in range(4):
        for copy in core_copies[g]:
            copy.wait_recv()

        @pl.loop(0, 16)
        def _(i):
            mine[g * 4 + lax.div(i, 4), lax.rem(i, 4)] += decode(
                core_in[g, i], core_scale_in[g, i]
            )

    first_x = ring(0, "x", 4, lambda there, half, i: mine[i * 4 + there, half])
    first_y = ring(1, "y", 4, lambda there, half, i: mine[there * 4 + i, 2 + half])
    first_x.start()
    first_y.start()

    def keep_list(half, i, total):
        list_sum[half * 4 + i] = total

    list_ring.finish(keep_list)

    @pl.loop(0, 8)
    def _(j):
        code, scale = encode(list_sum[j])
        list_out[j] = code
        list_scale_out[j] = scale

    here = lax.div(d, 4)

    def list_copies(j, out):
        to = here if out else j
        return (
            peer_copy(place, list_out.at[j], list_in.at[to], j, far_send, far_recv, out),
            peer_copy(
                place, list_scale_out.at[j], list_scale_in.at[to], j, far_send2, far_recv2, out
            ),
        )

    for j in range(8):

        @pl.when(j * 4 + share != d)
        def _():
            for copy in list_copies(j, True):
                copy.start()

        @pl.when(j * 4 + share == d)
        def _():
            list_in[j] = list_out[j]
            list_scale_in[j] = list_scale_out[j]

    first_x.relay()
    first_y.relay()

    def keep_num(half, i, total):
        num_out[half * 2 + i] = total

    num_ring.finish(keep_num)

    def keep_x(half, i, total):
        line_x[i, half] = total

    def keep_y(half, i, total):
        line_y[i, half] = total

    first_x.finish(keep_x)
    first_y.finish(keep_y)
    second_x = ring(2, "y", 1, lambda there, half, i: line_x[there, half])
    second_y = ring(3, "x", 1, lambda there, half, i: line_y[there, half])
    second_x.start()
    second_y.start()

    for j in range(8):

        @pl.when(j * 4 + share != d)
        def _():
            for copy in list_copies(j, False):
                copy.wait_recv()
                copy.wait_send()

        halo_out[j] = decode(list_in[j], list_scale_in[j]).T

    second_x.relay()
    second_y.relay()

    def keep_first(half, i, total):
        hub_out[half] = total.T

    def keep_second(half, i, total):
        hub_out[2 + half] = total.T

    second_x.finish(keep_first)
    second_y.finish(keep_second)
    links.drain()


def owners(far, num):
    tile = (BLK, BLK)
    one = (1, BLK)
    return pl.pallas_call(
        owners_body,
        in_specs=[ANY, ANY],
        out_specs=[VMEM, VMEM, VMEM],
        out_shape=[
            jax.ShapeDtypeStruct((4,) + tile, F32),
            jax.ShapeDtypeStruct((8,) + tile, F32),
            jax.ShapeDtypeStruct((4,) + tile, F32),
        ],
        scratch_shapes=[
            pltpu.VMEM((16, 4) + tile, F32),
            pltpu.VMEM((16, 4) + tile, F32),
            pltpu.VMEM((32,) + tile, F32),
            pltpu.VMEM((16,) + tile, F32),
            pltpu.VMEM((4, 16) + tile, I16),
            pltpu.VMEM((4, 16) + one, F32),
            pltpu.VMEM((4, 16) + tile, I16),
            pltpu.VMEM((4, 16) + one, F32),
            *ring_scratch(4, True),
            *ring_scratch(4, True),
            *ring_scratch(1, True),
            *ring_scratch(1, True),
            *ring_scratch(4, True),
            *ring_scratch(2, False),
            pltpu.VMEM((4, 2) + tile, F32),
            pltpu.VMEM((4, 2) + tile, F32),
            pltpu.VMEM((8,) + tile, F32),
            pltpu.VMEM((8,) + tile, I16),
            pltpu.VMEM((8,) + one, F32),
            pltpu.VMEM((8,) + tile, I16),
            pltpu.VMEM((8,) + one, F32),
            DMA((7,)),
            DMA((80,)),
            DMA((80,)),
            DMA((8,)),
            DMA((8,)),
            DMA((8,)),
            DMA((8,)),
        ],
        compiler_params=remote_params(1),
    )(far, num.reshape(-1, BLK, BLK))


def settle_body(
    idx, live, where, own, hub, halo, num, deg, feats, grads, w_self, w_neigh, bias,
    own_out, layer, weights, table, self_rows, sem,
):
    share = lax.axis_index("esplit")
    step = own.shape[0] // 4
    loads = []
    for g in range(4):
        part = pl.ds(g * step, step)
        loads.append(pltpu.make_async_copy(own.at[part], table.at[part], sem.at[g]))
    first = pl.multiple_of(where[0], 128)
    loads.append(pltpu.make_async_copy(feats.at[pl.ds(first, 512)], self_rows, sem.at[4]))
    for load in loads:
        load.start()

    at = pl.multiple_of(share * 512, 512)
    my_grads = grads[pl.ds(at, 512), :]
    wide = my_grads.astype(F32)
    loads[4].wait()
    mine = self_rows[...]
    contract = (((0,), (0,)), ((), ()))
    weights[0:128, :] = lax.dot_general(mine, my_grads, contract, preferred_element_type=F32)
    neigh = jnp.zeros((128, 128), F32)
    for i in range(4):
        divisor = jnp.maximum(deg[pl.ds(share * 4 + i, 1), :], 1.0)
        aggregate = num[i] / jnp.broadcast_to(divisor, (128, 128)).T
        rows = slice(i * 128, (i + 1) * 128)
        layer[rows, :] = (
            jnp.dot(
                aggregate,
                w_neigh[...].astype(F32),
                precision=lax.Precision.HIGHEST,
                preferred_element_type=F32,
            )
            + jnp.dot(mine[rows], w_self[...], preferred_element_type=F32)
            + bias[...].astype(F32)
        ).astype(BF16)
        neigh = neigh + lax.dot_general(
            aggregate, wide[rows], contract,
            precision=lax.Precision.HIGHEST, preferred_element_type=F32,
        )
    weights[128:256, :] = neigh
    weights[256:264, :] = jnp.broadcast_to(jnp.sum(wide, axis=0, keepdims=True), (8, 128))
    for j in range(8):
        row = lax.broadcasted_iota(I32, (128, 128), 0)
        halo[pl.ds(j * 128, 128), :] = jnp.where(
            row < live[j], halo[pl.ds(j * 128, 128), :], 0.0
        )
    back = lax.dot_general(
        my_grads, w_self[...], (((1,), (1,)), ((), ())), preferred_element_type=F32
    )
    for load in loads[:4]:
        load.wait()
    table[pl.ds(first, 512), :] += back

    def scatter(rows, base, count):
        @pl.loop(0, count // 8)
        def _(g):
            places = [idx[base + g * 8 + i] for i in range(8)]
            values = [
                table[pl.ds(places[i], 1), :] + rows[pl.ds(g * 8 + i, 1), :] for i in range(8)
            ]
            for i in range(8):
                table[pl.ds(places[i], 1), :] = values[i]

    scatter(hub, 0, 512)
    for j in range(8):
        scatter(halo.at[pl.ds(j * 128, 128)], 512 + j * 128, 128)
    outs = []
    for g in range(4):
        part = pl.ds(g * step, step)
        outs.append(pltpu.make_async_copy(table.at[part], own_out.at[part], sem.at[g]))
        outs[-1].start()
    for out in outs:
        out.wait()


def settle(idx, live, where, own, hub, halo, num, deg, feats, grads, w_self, w_neigh, bias):
    return pl.pallas_call(
        settle_body,
        in_specs=[SMEM, SMEM, SMEM, ANY, VMEM, VMEM, VMEM, VMEM, ANY, VMEM, VMEM, VMEM, VMEM],
        out_specs=[ANY, VMEM, VMEM],
        out_shape=[
            jax.ShapeDtypeStruct(own.shape, F32),
            jax.ShapeDtypeStruct((512, 128), BF16),
            jax.ShapeDtypeStruct((264, 128), F32),
        ],
        scratch_shapes=[pltpu.VMEM(own.shape, F32), pltpu.VMEM((512, 128), BF16), DMA((5,))],
        compiler_params=PARAMS,
    )(idx, live, where, own, hub, halo, num, deg, feats, grads, w_self, w_neigh, bias)


def final_body(own, weights, out, weights_out, table, *rest):
    rings = []
    for _ in range(4):
        rings.append(ring_bufs(rest[:4], True))
        rest = rest[4:]
    sums, slots, load_sem, out_sem, send_sem, recv_sem = rest
    place = Place()
    links = Links(send_sem, recv_sem)
    z = place.z
    loads = []
    for i, by in enumerate((2, 1, -1, 0)):
        part = pl.ds(place.step("z", by) * 32, 32)
        loads.append(pltpu.make_async_copy(own.at[part], table.at[part], load_sem.at[i]))
        loads[-1].start()
    near = [(axis, by) for axis in ("x", "y", "z") for by in (1, -1, 2)] + [("core", 1)]
    greet(place, near)

    def load(g):
        return lambda there, half, i: table[there * 32 + half * 16 + g * 4 + i]

    flows = [RingSum(place, links, "z", 4, load(g), *rings[g]) for g in range(4)]
    for stage in range(3):
        loads[stage].wait()
    for flow in flows:
        flow.start()

    def all_sum(stage, axis):
        mine = place.core if axis == "core" else place.at(axis)
        there = [1] if axis == "core" else [1, -1, 2]
        copies = [
            links.send(sums.at[stage], slots.at[stage, mine], place.device(axis, by))
            for by in there
        ]
        slots[stage, mine] = sums[stage]

        def end():
            for copy in copies:
                copy.wait_recv()
            total = slots[stage, 0] + slots[stage, 1]
            if axis != "core":
                total = total + (slots[stage, 2] + slots[stage, 3])
            if stage == 3:
                weights_out[...] = total
            else:
                sums[stage + 1] = total

        return end

    sums[0] = weights[...]
    end = all_sum(0, "core")
    flows[0].relay()
    end()
    end = all_sum(1, "x")
    flows[1].relay()
    flows[2].relay()
    end()
    end = all_sum(2, "y")
    flows[3].relay()
    end()
    end = all_sum(3, "z")
    loads[3].wait()
    outs = []
    for g in range(4):

        def store(half, i, total, g=g):
            table[z * 32 + half * 16 + g * 4 + i] = total

        flows[g].finish(store)
        for half in range(2):
            outs.append(
                pltpu.make_async_copy(
                    table.at[pl.ds(z * 32 + half * 16 + g * 4, 4)],
                    out.at[pl.ds(half * 16 + g * 4, 4)],
                    out_sem.at[g * 2 + half],
                )
            )
            outs[-1].start()
    end()
    for copy in outs:
        copy.wait()
    links.drain()


def final(own, weights):
    tile = (BLK, BLK)
    scratch = []
    for _ in range(4):
        scratch += ring_scratch(4, True)
    return pl.pallas_call(
        final_body,
        in_specs=[ANY, VMEM],
        out_specs=[ANY, VMEM],
        out_shape=[
            jax.ShapeDtypeStruct((32,) + tile, F32),
            jax.ShapeDtypeStruct(weights.shape, F32),
        ],
        scratch_shapes=[
            pltpu.VMEM((128,) + tile, F32),
            *scratch,
            pltpu.VMEM((4,) + weights.shape, F32),
            pltpu.VMEM((4, 4) + weights.shape, F32),
            DMA((4,)),
            DMA((8,)),
            DMA((64,)),
            DMA((64,)),
        ],
        compiler_params=remote_params(2),
    )(own, weights)


def local(
    features,
    adjacency,
    tile_source,
    hub_rows,
    send_rows,
    send_live,
    target_block,
    w_self,
    w_neigh,
    out_bias,
    out_grad,
):
    own_count, feat = features.shape
    peers = lax.axis_size("dom")
    d = lax.axis_index("dom")
    z = lax.axis_index("esplit")
    adj = adjacency[0, 0]
    src = tile_source[0, 0]
    blocks, rows, _, cols = adj.shape
    targets = blocks * rows
    hub_idx = hub_rows[0]
    hubs = hub_idx.shape[0]
    share = lax.rem(z - d + peers, 4)
    slots = send_rows.shape[2]
    lists = lax.dynamic_index_in_dim(send_rows[0].reshape(8, 4, slots), share, 1, keepdims=False)
    live = lax.dynamic_index_in_dim(send_live[0].reshape(8, 4), share, 1, keepdims=False)
    idx = jnp.concatenate([hub_idx, lists.reshape(-1)])
    picked = features[idx]
    hub_local = picked[:hubs]
    alive = jnp.arange(slots, dtype=I32)[None, :] < live[:, None]
    halo_local = jnp.where(
        alive[:, :, None], picked[hubs:].reshape(8, slots, feat), jnp.zeros((), features.dtype)
    )
    deg, hub_all, halo_all = exchange(adj, hub_local, halo_local)
    own, far, num = products(
        src,
        adj,
        out_grad,
        w_neigh,
        deg,
        features.reshape(-1, cols, feat),
        hub_all.reshape(-1, cols, feat),
        halo_all.reshape(-1, cols, feat),
    )
    hub_grad, halo_grad, num_sum = owners(far, num)
    where = target_block * rows + z * (targets // 4)
    own, layer, weights = settle(
        idx,
        live,
        where,
        own.reshape(-1, feat),
        hub_grad.reshape(-1, feat),
        halo_grad.reshape(-1, feat),
        num_sum,
        deg,
        features,
        out_grad,
        w_self,
        w_neigh,
        out_bias[None, :],
    )
    grad_features, weights = final(own.reshape(-1, BLK, feat), weights)
    weights = weights / math.sqrt(targets * peers)
    return (
        layer,
        grad_features.reshape(-1, feat),
        weights[:feat],
        weights[feat : 2 * feat],
        weights[2 * feat],
    )


def solution(mesh):
    in_specs = (
        P("dom", None),
        P("dom", "esplit", None, None, None, None),
        P("dom", "esplit", None, None),
        P("dom", None),
        P("dom", None, None),
        P("dom", None),
        P("dom"),
        P(),
        P(),
        P(),
        P("dom", None),
    )
    out_specs = (P(("dom", "esplit"), None), P(("dom", "esplit"), None), P(), P(), P())
    return jax.shard_map(local, mesh=mesh, in_specs=in_specs, out_specs=out_specs, check_vma=False)
```

time: 523 us -> 185 us (0.35)
  waiting for transfers between devices: 325 us -> 0 us
  Pallas kernels: 59.8 us -> 167 us
  other arithmetic: 55.1 us -> 4.54 us
  local copies, waits for them, and re-layouts: 33.7 us -> 11.8 us
  starting transfers between devices: 15.1 us -> 0 us
  between operations: 14.6 us -> 1.42 us
  blocking collectives: 11.9 us -> 0 us
  matrix products: 6.5 us -> 0 us
    all_gather x1 -> x0, waiting for transfers between devices: 123 us -> none  [local(): hub_all = lax.all_gather(hub_local, 'dom', axis=0, tiled=True)]
    pallas_call x3 -> x5, Pallas kernels: 59.8 us -> 167 us  [the longest x1 45.9 us: final(): pl.pallas_call(final_body, in_specs=[ANY, VMEM], out_specs=[ANY, VMEM], o...]
    psum x1 -> x0, waiting for transfers between devices: 102 us -> none  [local(): lax.psum(weight_grads, ('dom', 'esplit')) / math.sqrt(targets * peers)]
    reduce_scatter x2 -> x0, waiting for transfers between devices: 99.9 us -> none  [the longest x1 78.8 us: local(): lax.psum_scatter(own_grad, 'esplit', scatter_dimension=0, tiled=True)]
    scatter-add x2 -> x0, other arithmetic: 36.3 us -> none  [the longest x1 26.7 us: local(): own_grad.at[lists].add(jnp.where(live[:, :, None], returned[:, hubs:], 0.0))]
    all_to_all x2 -> x0, starting transfers between devices: 14.9 us -> none  [the longest x1 7.49 us: local(): lax.all_to_all(packet, 'dom', split_axis=0, concat_axis=0, tiled=True)]
    gather x2 -> x1, local copies, waits for them, and re-layouts: 18.1 us -> 5.37 us  [local(): picked = features[idx]]
    psum x1 -> x0, blocking collectives: 11.9 us -> none  [local(): deg = lax.psum(degree_part(adj)[:, :1], 'esplit')]
  transfers between devices with their start and end apart: 6 -> 0, of which waited for: 4 -> 0; matrix products, arithmetic and copies ran while one was open for 14% -> 0% of each run, Pallas kernels for 11% -> 0%
where the time goes in v2:
time: 185 us
  Pallas kernels  167 us (90%)
  local copies, waits for them, and re-layouts  11.8 us (6%)
  other arithmetic  4.54 us (2%)
    pallas_call x1, Pallas kernels, final(): pl.pallas_call(final_body, in_specs=[ANY, VMEM], out_specs=[ANY, VMEM], o...  45.9 us
    pallas_call x1, Pallas kernels, owners(): pl.pallas_call(owners_body, in_specs=[ANY, ANY], out_specs=[VMEM, VMEM, V...  43.5 us
    pallas_call x1, Pallas kernels, exchange(): pl.pallas_call(exchange_body, in_specs=[ANY, ANY, ANY], out_specs=[VMEM,...  33.2 us
    pallas_call x1, Pallas kernels, products(): pl.pallas_call(products_body, in_specs=[SMEM, ANY, VMEM, VMEM, VMEM, ANY,...  32.2 us
    pallas_call x1, Pallas kernels, settle(): pl.pallas_call(settle_body, in_specs=[SMEM, SMEM, SMEM, ANY, VMEM, VMEM,...  12.3 us
    gather x1, local copies, waits for them, and re-layouts, local(): picked = features[idx]  5.37 us
    unnamed x8, local copies, waits for them, and re-layouts  4.27 us

profile of v2, /device:TPU:0, one launch (start us, length us, event | category | flops | bytes accessed | tf_op | source)
XLA Modules:
  0.0 184.7 jit_solution(4870208813233431777)
XLA Ops:
  0.6 0.0 copy-start
  0.7 0.7 copy-done
  1.4 0.7 fusion
  2.1 5.4 %gather_fusion = bf16[1536,128]{1,0:T(8,128)(2,1)S(1)} fusion(bf16[16384,128]{1,0:T(8,128)(2,1)} %feats.1, s32[2048]{0:T(1024)S(1)} %pad_clamp_fusion), kind=kCustom, calls=%fused_computation | custom fusion | bytes 792576 | tf_op jit(solution)/shard_map/gather | solution.py:908
  7.5 0.5 broadcast.39
  8.0 1.3 reduce.7
  9.3 0.1 reshape_squeeze.7
  9.4 0.2 dynamic-slice_reduce_fusion.live
  9.6 0.0 copy-start.2
  9.6 0.1 iota_compare_fusion
  9.7 0.9 broadcast_select_fusion.halo_in
  10.6 0.7 slice.22
  11.3 33.2 %shard_map.146 = (f32[16,128]{1,0:T(8,128)}, bf16[4,4,2,2,256,128]{5,4,3,2,1,0:T(8,128)(2,1)}, bf16[8,4,128,128]{3,2,1,0:T(8,128)(2,1)}) custom-call(bf16[16,128,32,128]{3,2,1,0:T(8,128)(2,1)} %bitcast.25, bf16[2,256,128]{2,1,0:T(8,128)(2,1)} %bitcast.36, bf16[8,128,128]{2,1,0:T(8,128)(2,1)} %broadcast_select_fusion.halo_in), custom_call_target="tpu_custom_call" | custom-call | tf_op jit(solution)/shard_map/pallas_call | solution.py:251
  44.4 0.0 copy-done.2
  44.4 32.2 %shard_map.147 = (f32[128,128,128]{2,1,0:T(8,128)}, f32[160,128,128]{2,1,0:T(8,128)}, f32[2048,128]{1,0:T(8,128)}) custom-call(s32[16,32]{1,0:T(8,128)} %bitcast.39, bf16[16,128,32,128]{3,2,1,0:T(8,128)(2,1)} %bitcast.26, bf16[2048,128]{1,0:T(8,128)(2,1)} %grads.3, bf16[128,128]{1,0:T(8,128)(2,1)} %w_neigh.3, f32[16,128]{1,0:T(8,128)} %get-tuple-element.19.deg, ...), custom_call_target="tpu_custom_call" | custom-call | tf_op jit(solution)/shard_map/pallas_call | solution.py:354
  76.6 0.0 copy-start.1
  76.6 43.5 %shard_map.148 = (f32[4,128,128]{2,1,0:T(8,128)}, f32[8,128,128]{2,1,0:T(8,128)}, f32[4,128,128]{2,1,0:T(8,128)}) custom-call(f32[160,128,128]{2,1,0:T(8,128)} %get-tuple-element.23.far, f32[16,128,128]{2,1,0:T(8,128)} %bitcast.34), custom_call_target="tpu_custom_call" | custom-call | tf_op jit(solution)/shard_map/pallas_call | solution.py:635
  120.1 0.0 copy-done.1
  120.1 0.6 pad_add_fusion.idx
  121.4 12.3 %shard_map.149 = (f32[16384,128]{1,0:T(8,128)}, bf16[512,128]{1,0:T(8,128)(2,1)}, f32[264,128]{1,0:T(8,128)}) custom-call(s32[1536]{0:T(1024)} %pad_add_fusion.idx, s32[8]{0:T(128)} %copy-done.2, s32[1]{0:T(128)S(6)} %add.31.where, f32[16384,128]{1,0:T(8,128)} %bitcast.28, f32[512,128]{1,0:T(8,128)} %bitcast.37, f32[1024,128]{1,0:T(8,128)} %bitcast.35, ...), custom_call_target="tpu_custom_call" | custom-call | tf_op jit(solution)/shard_map/pallas_call | solution.py:756
  133.7 45.9 %shard_map.150 = (f32[32,128,128]{2,1,0:T(8,128)}, f32[264,128]{1,0:T(8,128)}) custom-call(f32[128,128,128]{2,1,0:T(8,128)} %bitcast.29, f32[264,128]{1,0:T(8,128)} %get-tuple-element.30.weights), custom_call_target="tpu_custom_call" | custom-call | tf_op jit(solution)/shard_map/pallas_call | solution.py:858
  179.6 0.9 broadcast_multiply_fusion
  180.5 0.7 fusion.1
  181.2 0.5 slice_bitcast_fusion
  181.7 3.0 %copy.18 = f32[4096,128]{1,0:T(8,128)} copy(f32[4096,128]{1,0:T(8,128)} %bitcast.31) | data formatting | bytes 4194304
  (4 shorter events, 0.0 us)
Async XLA Ops:
  0.6 0.7 copy-start
  9.6 34.8 %copy-start.2 = (s32[8]{0:T(128)}, s32[8]{0:T(128)S(1)}, u32[]{:S(2)}) copy-start(s32[8]{0:T(128)S(1)} %dynamic-slice_reduce_fusion.live) | copy-start | bytes 100
  76.6 43.5 %copy-start.1 = (s32[1,512]{1,0:T(1,128)S(1)}, s32[1,512]{1,0:T(1,128)}, u32[]{:S(2)}) copy-start(s32[1,512]{1,0:T(1,128)} %param.14) | copy-start | bytes 6148

commit v3 on v2

--- a/solution.py
+++ b/solution.py
@@ -61,6 +61,7 @@
         self.send_sem, self.recv_sem, self.used, self.made = send_sem, recv_sem, 0, []
 
     def send(self, src, dst, device):
+        assert self.used < self.send_sem.shape[0]
         copy = pltpu.make_async_remote_copy(
             src_ref=src,
             dst_ref=dst,
@@ -97,10 +98,12 @@
                     barrier, inc=1, device_id=(peer, place.z), device_id_type=MESH
                 )
 
-        mine = (lax.rem(place.d, 4) == share).astype(I32)
-        pl.semaphore_wait(barrier, count + 8 - mine)
-    else:
+        count = count + 8 - (lax.rem(place.d, 4) == share).astype(I32)
+
+    def wait():
         pl.semaphore_wait(barrier, count)
+
+    return wait
 
 
 def peer_copy(place, src, dst, j, send_sem, recv_sem, out):
@@ -126,33 +129,13 @@
     x, y, c, d, z = place.x, place.y, place.core, place.d, place.z
     share = place.share()
     blocks = adj.shape[0]
+    near = [("x", 1), ("x", -1), ("y", 1), ("y", -1), ("z", 1), ("z", -1), ("z", 2), ("core", 1)]
+    ready = greet(place, near, far=True)
     for b in range(blocks):
         block_copy(adj, buf, adj_sem, b).start()
     own_hub = pltpu.make_async_copy(hub_in, hub_out.at[y, x, c], local_sem.at[0])
     own_hub.start()
-    near = [("x", 1), ("x", -1), ("y", 1), ("y", -1), ("z", 1), ("z", -1), ("z", 2), ("core", 1)]
-    greet(place, near, far=True)
     links = Links(send_sem, recv_sem)
-
-    first = {}
-    for axis, half in (("x", 0), ("y", 1)):
-        for by in (1, -1):
-            first[axis, by] = links.send(
-                hub_in.at[half], hub_out.at[y, x, c, half], place.device(axis, by)
-            )
-    here = lax.div(d, 4)
-    for j in range(8):
-
-        @pl.when(j * 4 + share != d)
-        def _():
-            there = halo_out.at[here, lax.rem(d, 4)]
-            peer_copy(place, halo_in.at[j], there, j, far_send, far_recv, True).start()
-
-        @pl.when(j * 4 + share == d)
-        def _():
-            keep = pltpu.make_async_copy(halo_in.at[j], halo_out.at[j, share], local_sem.at[1])
-            keep.start()
-            keep.wait()
 
     def degrees(low, high):
         @pl.loop(low, high)
@@ -168,33 +151,78 @@
             )
             deg_mine[pl.ds(b, 1), :] = rows[0:1]
 
-    degrees(0, 4)
-    relay = {}
-    for axis, half in (("x", 0), ("y", 1)):
+    flows = (("x", "y", 0), ("y", "x", 1))
+    cores = []
+
+    def piece(flow, along, across, rows=None):
+        axis, other, half = flow
+        p, q = place.step(axis, along), place.step(other, across)
+        at = (q, p) if axis == "x" else (p, q)
+        if rows is None:
+            return hub_out.at[at[0], at[1], c, half]
+        return hub_out.at[at[0], at[1], c, half, pl.ds(rows * 128, 128)]
+
+    def pass_on(ref, axis, by):
+        return links.send(ref, ref, place.device(axis, by))
+
+    def to_core(ref):
+        cores.append(pass_on(ref, "core", 1))
+
+    first, relay, second, third = {}, {}, {}, {}
+    degrees(0, 1)
+    ready()
+    for flow in flows:
+        axis, other, half = flow
+        for by in (1, -1):
+            first[axis, by] = links.send(
+                hub_in.at[half], piece(flow, 0, 0), place.device(axis, by)
+            )
+    here = lax.div(d, 4)
+    for j in range(8):
+
+        @pl.when(j * 4 + share != d)
+        def _():
+            there = halo_out.at[here, lax.rem(d, 4)]
+            peer_copy(place, halo_in.at[j], there, j, far_send, far_recv, True).start()
+
+        @pl.when(j * 4 + share == d)
+        def _():
+            keep = pltpu.make_async_copy(halo_in.at[j], halo_out.at[j, share], local_sem.at[1])
+            keep.start()
+            keep.wait()
+
+    for flow in flows:
+        axis, other, half = flow
+        for by in (1, -1):
+            second[axis, 0, by] = links.send(
+                hub_in.at[half], piece(flow, 0, 0), place.device(other, by)
+            )
+    degrees(1, 4)
+    own_hub.wait()
+    for flow in flows:
+        to_core(piece(flow, 0, 0))
+        axis, other, half = flow
         for by, part in ((1, 0), (-1, 1)):
             first[axis, by].wait_recv()
-            back = place.step(axis, -by)
-            at = (y, back) if axis == "x" else (back, x)
-            piece = hub_out.at[at[0], at[1], c, half, pl.ds(part * 128, 128)]
-            relay[axis, by] = links.send(piece, piece, place.device(axis, by))
-    degrees(4, blocks)
-    deg_all[z] = deg_mine[...]
-    deg_copies = [
-        links.send(deg_mine, deg_all.at[z], place.device("z", by)) for by in (1, -1, 2)
-    ]
-
-    own_hub.wait()
-    second = {}
-    for axis, other, half in (("x", "y", 0), ("y", "x", 1)):
-        relay[axis, 1].wait_recv()
-        relay[axis, -1].wait_recv()
-        line = hub_out.at[y, :, c, half] if axis == "x" else hub_out.at[:, x, c, half]
+            relay[axis, by] = pass_on(piece(flow, -by, 0, part), axis, by)
+        for along in (-1, 1):
+            for by in (1, -1):
+                second[axis, along, by] = pass_on(piece(flow, along, 0), other, by)
+            to_core(piece(flow, along, 0))
+
+    def carry(flow, along):
+        axis, other, half = flow
+        forward = 1 if along in (0, 2) else -1
         for by in (1, -1):
-            second[other, by] = links.send(line, line, place.device(other, by))
-    for axis, half in (("x", 0), ("y", 1)):
-        line = hub_out.at[y, :, c, half] if axis == "x" else hub_out.at[:, x, c, half]
-        second["core", axis] = links.send(line, line, place.device("core", 1))
-
+            second[axis, along, by].wait_recv()
+            if by == forward:
+                third[axis, along] = pass_on(piece(flow, along, -by), other, by)
+            to_core(piece(flow, along, -by))
+
+    degrees(4, 7)
+    for flow in flows:
+        carry(flow, 0)
+    halo_first, halo_relay = {}, []
     for j in range(8):
 
         @pl.when(j * 4 + share != d)
@@ -205,42 +233,39 @@
             come.wait_recv()
             come.wait_send()
 
-    mine = halo_out.at[:, share]
-    halo_first = {by: links.send(mine, mine, place.device("z", by)) for by in (1, -1)}
-
-    third = {}
-    last = []
-    for axis, other, half in (("x", "y", 0), ("y", "x", 1)):
-        for by, part in ((1, 0), (-1, 1)):
-            second[other, by].wait_recv()
-            back = place.step(other, -by)
-            if axis == "x":
-                line = hub_out.at[back, :, c, half]
-                piece = hub_out.at[back, pl.ds(part * 2, 2), c, half]
-            else:
-                line = hub_out.at[:, back, c, half]
-                piece = hub_out.at[pl.ds(part * 2, 2), back, c, half]
-            third[other, by] = links.send(piece, piece, place.device(other, by))
-            last.append(links.send(line, line, place.device("core", 1)))
-
-    halo_relay = []
-    for by, part in ((1, 0), (-1, 1)):
-        halo_first[by].wait_recv()
-        back = lax.rem(place.step("z", -by) - d + 32, 4)
-        piece = halo_out.at[pl.ds(part * 4, 4), back]
-        halo_relay.append(links.send(piece, piece, place.device("z", by)))
-
-    for axis, other, half in (("x", "y", 0), ("y", "x", 1)):
-        third[other, 1].wait_recv()
-        third[other, -1].wait_recv()
-        back = place.step(other, 2)
-        line = hub_out.at[back, :, c, half] if axis == "x" else hub_out.at[:, back, c, half]
-        last.append(links.send(line, line, place.device("core", 1)))
-
+        for by in (1, -1):
+            halo_first[j, by] = pass_on(halo_out.at[j, share], "z", by)
+    for flow in flows:
+        axis, other, half = flow
+        relay[axis, 1].wait_recv()
+        relay[axis, -1].wait_recv()
+        for by in (1, -1):
+            second[axis, 2, by] = pass_on(piece(flow, 2, 0), other, by)
+        to_core(piece(flow, 2, 0))
+    degrees(7, blocks)
+    deg_all[z] = deg_mine[...]
+    deg_copies = [
+        links.send(deg_mine, deg_all.at[z], place.device("z", by)) for by in (1, -1, 2)
+    ]
+    for along in (-1, 1):
+        for flow in flows:
+            carry(flow, along)
+    for j in range(8):
+        for by in (1, -1):
+            halo_first[j, by].wait_recv()
+            if (by == 1) == (j % 2 == 0):
+                back = lax.rem(place.step("z", -by) - d + 32, 4)
+                halo_relay.append(pass_on(halo_out.at[j, back], "z", by))
+    for flow in flows:
+        carry(flow, 2)
+    for along in (0, -1, 1, 2):
+        for flow in flows:
+            third[flow[0], along].wait_recv()
+            to_core(piece(flow, along, 2))
     for copy in deg_copies:
         copy.wait_recv()
     deg_out[...] = (deg_all[0] + deg_all[1]) + (deg_all[2] + deg_all[3])
-    for copy in halo_relay + last + [second["core", "x"], second["core", "y"]]:
+    for copy in halo_relay + cores:
         copy.wait_recv()
     links.drain()
 
@@ -263,8 +288,8 @@
             pltpu.VMEM((blocks, rows), F32),
             DMA((blocks,)),
             DMA((2,)),
-            DMA((32,)),
-            DMA((32,)),
+            DMA((96,)),
+            DMA((96,)),
             DMA((8,)),
             DMA((8,)),
         ],
@@ -412,7 +437,7 @@
         self.copies = {}
 
     def push(self, m, by, block):
-        @pl.loop(0, self.count)
+        @pl.loop(0, self.count, unroll=min(2, self.count))
         def _(i):
             self.out[m].put(i, block(i))
 
@@ -424,13 +449,20 @@
         for copy in self.copies[m]:
             copy.wait_recv()
 
+    def start_opposite(self):
+        there = self.place.step(self.axis, 2)
+        for m, by, half in ((0, 1, 0), (1, -1, 1)):
+            self.push(m, by, lambda i, half=half: self.load(there, half, i))
+
+    def start_near(self, by):
+        m, half = (2, 1) if by == 1 else (3, 0)
+        there = self.place.step(self.axis, by)
+        self.push(m, by, lambda i: self.load(there, half, i))
+
     def start(self):
-        opposite = self.place.step(self.axis, 2)
-        for m, by, half in ((0, 1, 0), (1, -1, 1)):
-            self.push(m, by, lambda i, half=half: self.load(opposite, half, i))
-        for m, by, half in ((2, 1, 1), (3, -1, 0)):
-            there = self.place.step(self.axis, by)
-            self.push(m, by, lambda i, there=there, half=half: self.load(there, half, i))
+        self.start_opposite()
+        self.start_near(1)
+        self.start_near(-1)
 
     def relay(self):
         for m, by, half in ((4, 1, 0), (5, -1, 1)):
@@ -449,7 +481,7 @@
             self.wait(a)
             self.wait(b)
 
-            @pl.loop(0, self.count)
+            @pl.loop(0, self.count, unroll=min(2, self.count))
             def _(i):
                 store(
                     half,
@@ -485,22 +517,34 @@
     share = place.share()
     links = Links(send_sem, recv_sem)
 
-    hub_far = far.at[pl.ds(0, 128)].reshape(16, 2, 4, BLK, BLK)
-    loads = [
-        pltpu.make_async_copy(far.at[pl.ds(128, 32)], lists, load_sem.at[0]),
-        pltpu.make_async_copy(num_in, num, load_sem.at[1]),
-    ]
-    for g in range(4):
-        loads.append(
-            pltpu.make_async_copy(
-                hub_far.at[pl.ds(g * 4, 4), 1 - c], theirs.at[pl.ds(g * 4, 4)], load_sem.at[2 + g]
-            )
-        )
-    loads.append(pltpu.make_async_copy(hub_far.at[:, c], mine, load_sem.at[6]))
-    for load in loads:
-        load.start()
     near = [("x", 1), ("x", -1), ("y", 1), ("y", -1), ("z", 1), ("z", -1), ("core", 1)]
-    greet(place, near, far=True)
+    ready = greet(place, near, far=True)
+    hub_far = far.at[pl.ds(0, 128)].reshape(4, 4, 2, 4, BLK, BLK)
+
+    def part_of(g):
+        by = (2, 1, -1, 0)[g // 2]
+        if g % 2 == 0:
+            return slice(None), place.step("x", by), pl.ds(0, 2)
+        return place.step("y", by), slice(None), pl.ds(2, 2)
+
+    def block_at(g, i):
+        by = (2, 1, -1, 0)[g // 2]
+        if g % 2 == 0:
+            return lax.div(i, 2), place.step("x", by), lax.rem(i, 2)
+        return place.step("y", by), lax.div(i, 2), 2 + lax.rem(i, 2)
+
+    loads = []
+
+    def load(src, dst):
+        loads.append(pltpu.make_async_copy(src, dst, load_sem.at[len(loads)]))
+        loads[-1].start()
+
+    for g in range(8):
+        p, q, t = part_of(g)
+        load(hub_far.at[p, q, 1 - c, t], theirs.at[p, q, t])
+    load(far.at[pl.ds(128, 32)], lists)
+    load(hub_far.at[:, :, c], mine)
+    load(num_in, num)
 
     def ring(which, axis, count, load):
         return RingSum(place, links, axis, count, load, *rings[which])
@@ -510,45 +554,61 @@
 
     list_ring = ring(4, "z", 4, list_for)
     num_ring = ring(5, "z", 2, lambda there, half, i: num[there * 4 + half * 2 + i])
-    loads[0].wait()
-    list_ring.start()
-    loads[1].wait()
-    num_ring.start()
-
+    first_x = ring(0, "x", 4, lambda there, half, i: mine[i, there, half])
+    first_y = ring(1, "y", 4, lambda there, half, i: mine[there, i, 2 + half])
     core_copies = []
-    for g in range(4):
-        loads[2 + g].wait()
-
-        @pl.loop(0, 16)
+    there = place.device("core", 1)
+    for g in range(8):
+        loads[g].wait()
+
+        @pl.loop(0, 8, unroll=2)
         def _(i):
-            code, scale = encode(theirs[g * 4 + lax.div(i, 4), lax.rem(i, 4)])
+            code, scale = encode(theirs[block_at(g, i)])
             core_out[g, i] = code
             core_scale_out[g, i] = scale
 
-        there = place.device("core", 1)
+        if g == 0:
+            ready()
         core_copies.append(
             [
                 links.send(core_out.at[g], core_in.at[g], there),
                 links.send(core_scale_out.at[g], core_scale_in.at[g], there),
             ]
         )
-    list_ring.relay()
-    num_ring.relay()
-    loads[6].wait()
-    for g in range(4):
+        if g == 1:
+            loads[8].wait()
+            list_ring.start()
+
+    loads[9].wait()
+
+    def merge(g):
         for copy in core_copies[g]:
             copy.wait_recv()
 
-        @pl.loop(0, 16)
+        @pl.loop(0, 8, unroll=2)
         def _(i):
-            mine[g * 4 + lax.div(i, 4), lax.rem(i, 4)] += decode(
-                core_in[g, i], core_scale_in[g, i]
-            )
-
-    first_x = ring(0, "x", 4, lambda there, half, i: mine[i * 4 + there, half])
-    first_y = ring(1, "y", 4, lambda there, half, i: mine[there * 4 + i, 2 + half])
-    first_x.start()
-    first_y.start()
+            at = block_at(g, i)
+            mine[at] = mine[at] + decode(core_in[g, i], core_scale_in[g, i])
+
+    merge(0)
+    first_x.start_opposite()
+    merge(1)
+    first_y.start_opposite()
+    merge(2)
+    first_x.start_near(1)
+    merge(3)
+    first_y.start_near(1)
+    merge(4)
+    first_x.start_near(-1)
+    merge(5)
+    first_y.start_near(-1)
+    list_ring.relay()
+    first_x.relay()
+    first_y.relay()
+    loads[10].wait()
+    num_ring.start()
+    merge(6)
+    merge(7)
 
     def keep_list(half, i, total):
         list_sum[half * 4 + i] = total
@@ -584,13 +644,7 @@
             list_in[j] = list_out[j]
             list_scale_in[j] = list_scale_out[j]
 
-    first_x.relay()
-    first_y.relay()
-
-    def keep_num(half, i, total):
-        num_out[half * 2 + i] = total
-
-    num_ring.finish(keep_num)
+    num_ring.relay()
 
     def keep_x(half, i, total):
         line_x[i, half] = total
@@ -617,6 +671,11 @@
 
     second_x.relay()
     second_y.relay()
+
+    def keep_num(half, i, total):
+        num_out[half * 2 + i] = total
+
+    num_ring.finish(keep_num)
 
     def keep_first(half, i, total):
         hub_out[half] = total.T
@@ -642,14 +701,14 @@
             jax.ShapeDtypeStruct((4,) + tile, F32),
         ],
         scratch_shapes=[
-            pltpu.VMEM((16, 4) + tile, F32),
-            pltpu.VMEM((16, 4) + tile, F32),
+            pltpu.VMEM((4, 4, 4) + tile, F32),
+            pltpu.VMEM((4, 4, 4) + tile, F32),
             pltpu.VMEM((32,) + tile, F32),
             pltpu.VMEM((16,) + tile, F32),
-            pltpu.VMEM((4, 16) + tile, I16),
-            pltpu.VMEM((4, 16) + one, F32),
-            pltpu.VMEM((4, 16) + tile, I16),
-            pltpu.VMEM((4, 16) + one, F32),
+            pltpu.VMEM((8, 8) + tile, I16),
+            pltpu.VMEM((8, 8) + one, F32),
+            pltpu.VMEM((8, 8) + tile, I16),
+            pltpu.VMEM((8, 8) + one, F32),
             *ring_scratch(4, True),
             *ring_scratch(4, True),
             *ring_scratch(1, True),
@@ -663,9 +722,9 @@
             pltpu.VMEM((8,) + one, F32),
             pltpu.VMEM((8,) + tile, I16),
             pltpu.VMEM((8,) + one, F32),
-            DMA((7,)),
-            DMA((80,)),
-            DMA((80,)),
+            DMA((11,)),
+            DMA((96,)),
+            DMA((96,)),
             DMA((8,)),
             DMA((8,)),
             DMA((8,)),
@@ -677,7 +736,7 @@
 
 def settle_body(
     idx, live, where, own, hub, halo, num, deg, feats, grads, w_self, w_neigh, bias,
-    own_out, layer, weights, table, self_rows, sem,
+    own_out, relay_out, codes, scales, layer, weights, table, self_rows, code, scale, sem, out_sem,
 ):
     share = lax.axis_index("esplit")
     step = own.shape[0] // 4
@@ -744,66 +803,101 @@
     for j in range(8):
         scatter(halo.at[pl.ds(j * 128, 128)], 512 + j * 128, 128)
     outs = []
-    for g in range(4):
-        part = pl.ds(g * step, step)
-        outs.append(pltpu.make_async_copy(table.at[part], own_out.at[part], sem.at[g]))
+
+    def put(src, dst):
+        outs.append(pltpu.make_async_copy(src, dst, out_sem.at[len(outs)]))
         outs[-1].start()
+
+    def rows_for(by, half):
+        quarter = lax.rem(share + (by + 4), 4)
+        return pl.multiple_of((quarter * 2 + half) * 2048, 2048)
+
+    put(table.at[pl.ds(rows_for(0, 0), 4096)], own_out)
+    put(table.at[pl.ds(rows_for(1, 0), 2048)], relay_out.at[0])
+    put(table.at[pl.ds(rows_for(-1, 1), 2048)], relay_out.at[1])
+    for m, by, half in ((0, 2, 0), (1, 2, 1), (2, 1, 1), (3, -1, 0)):
+        base = rows_for(by, half)
+
+        @pl.loop(0, 16, unroll=2)
+        def _(i):
+            rows = pl.ds(pl.multiple_of(base + i * BLK, BLK), BLK)
+            code[m, i], scale[m, i] = encode(table[rows, :])
+
+        put(code.at[m], codes.at[m])
+        put(scale.at[m], scales.at[m])
     for out in outs:
         out.wait()
 
 
 def settle(idx, live, where, own, hub, halo, num, deg, feats, grads, w_self, w_neigh, bias):
+    codes = (4, 16, BLK, BLK)
+    scales = (4, 16, 1, BLK)
     return pl.pallas_call(
         settle_body,
         in_specs=[SMEM, SMEM, SMEM, ANY, VMEM, VMEM, VMEM, VMEM, ANY, VMEM, VMEM, VMEM, VMEM],
-        out_specs=[ANY, VMEM, VMEM],
+        out_specs=[ANY, ANY, ANY, ANY, VMEM, VMEM],
         out_shape=[
-            jax.ShapeDtypeStruct(own.shape, F32),
+            jax.ShapeDtypeStruct((4096, 128), F32),
+            jax.ShapeDtypeStruct((2, 2048, 128), F32),
+            jax.ShapeDtypeStruct(codes, I16),
+            jax.ShapeDtypeStruct(scales, F32),
             jax.ShapeDtypeStruct((512, 128), BF16),
             jax.ShapeDtypeStruct((264, 128), F32),
         ],
-        scratch_shapes=[pltpu.VMEM(own.shape, F32), pltpu.VMEM((512, 128), BF16), DMA((5,))],
+        scratch_shapes=[
+            pltpu.VMEM(own.shape, F32),
+            pltpu.VMEM((512, 128), BF16),
+            pltpu.VMEM(codes, I16),
+            pltpu.VMEM(scales, F32),
+            DMA((5,)),
+            DMA((11,)),
+        ],
         compiler_params=PARAMS,
     )(idx, live, where, own, hub, halo, num, deg, feats, grads, w_self, w_neigh, bias)
 
 
-def final_body(own, weights, out, weights_out, table, *rest):
-    rings = []
-    for _ in range(4):
-        rings.append(ring_bufs(rest[:4], True))
-        rest = rest[4:]
-    sums, slots, load_sem, out_sem, send_sem, recv_sem = rest
+def final_body(
+    codes, scales, relay_in, weights, come, come_scale, weights_out,
+    far, far_scale, part, out, out_scale, sums, slots, load_sem, send_sem, recv_sem,
+):
     place = Place()
     links = Links(send_sem, recv_sem)
-    z = place.z
-    loads = []
-    for i, by in enumerate((2, 1, -1, 0)):
-        part = pl.ds(place.step("z", by) * 32, 32)
-        loads.append(pltpu.make_async_copy(own.at[part], table.at[part], load_sem.at[i]))
-        loads[-1].start()
     near = [(axis, by) for axis in ("x", "y", "z") for by in (1, -1, 2)] + [("core", 1)]
-    greet(place, near)
-
-    def load(g):
-        return lambda there, half, i: table[there * 32 + half * 16 + g * 4 + i]
-
-    flows = [RingSum(place, links, "z", 4, load(g), *rings[g]) for g in range(4)]
-    for stage in range(3):
-        loads[stage].wait()
-    for flow in flows:
-        flow.start()
+    ready = greet(place, near)
+    loads = [
+        pltpu.make_async_copy(relay_in.at[n], part.at[n], load_sem.at[n]) for n in range(2)
+    ]
+    for load in loads:
+        load.start()
+    ready()
+
+    def send(m, g, code, scale, to_code, to_scale):
+        there = place.device("z", 1 if m % 2 == 0 else -1)
+        return [
+            links.send(code, to_code, there),
+            links.send(scale, to_scale, there),
+        ]
+
+    copies = {}
+    quad = [pl.ds(g * 4, 4) for g in range(4)]
+    for g in range(4):
+        for m in (0, 1):
+            copies[m, g] = send(
+                m, g, codes.at[m, quad[g]], scales.at[m, quad[g]],
+                far.at[m, quad[g]], far_scale.at[m, quad[g]],
+            )
 
     def all_sum(stage, axis):
         mine = place.core if axis == "core" else place.at(axis)
         there = [1] if axis == "core" else [1, -1, 2]
-        copies = [
+        rounds = [
             links.send(sums.at[stage], slots.at[stage, mine], place.device(axis, by))
             for by in there
         ]
         slots[stage, mine] = sums[stage]
 
         def end():
-            for copy in copies:
+            for copy in rounds:
                 copy.wait_recv()
             total = slots[stage, 0] + slots[stage, 1]
             if axis != "core":
@@ -817,64 +911,113 @@
 
     sums[0] = weights[...]
     end = all_sum(0, "core")
-    flows[0].relay()
-    end()
-    end = all_sum(1, "x")
-    flows[1].relay()
-    flows[2].relay()
-    end()
-    end = all_sum(2, "y")
-    flows[3].relay()
-    end()
-    end = all_sum(3, "z")
-    loads[3].wait()
-    outs = []
     for g in range(4):
-
-        def store(half, i, total, g=g):
-            table[z * 32 + half * 16 + g * 4 + i] = total
-
-        flows[g].finish(store)
-        for half in range(2):
-            outs.append(
-                pltpu.make_async_copy(
-                    table.at[pl.ds(z * 32 + half * 16 + g * 4, 4)],
-                    out.at[pl.ds(half * 16 + g * 4, 4)],
-                    out_sem.at[g * 2 + half],
-                )
+        for m in (2, 3):
+            copies[m, g] = send(
+                m, g, codes.at[m, quad[g]], scales.at[m, quad[g]],
+                come.at[m - 2, quad[g]], come_scale.at[m - 2, quad[g]],
             )
-            outs[-1].start()
-    end()
-    for copy in outs:
-        copy.wait()
+    for load in loads:
+        load.wait()
+    for g in range(4):
+        for m in (0, 1):
+            for copy in copies[m, g]:
+                copy.wait_recv()
+
+            @pl.loop(g * 4, g * 4 + 4, unroll=2)
+            def _(i):
+                block = part[m, i] + decode(far[m, i], far_scale[m, i])
+                out[m, i], out_scale[m, i] = encode(block)
+
+            copies[m + 4, g] = send(
+                m, g, out.at[m, quad[g]], out_scale.at[m, quad[g]],
+                come.at[m + 2, quad[g]], come_scale.at[m + 2, quad[g]],
+            )
+        end()
+        if g < 3:
+            end = all_sum(g + 1, ("x", "y", "z")[g])
+    for m in (2, 3, 4, 5):
+        for g in range(4):
+            for copy in copies[m, g]:
+                copy.wait_recv()
     links.drain()
 
 
-def final(own, weights):
-    tile = (BLK, BLK)
-    scratch = []
-    for _ in range(4):
-        scratch += ring_scratch(4, True)
+def final(codes, scales, relay, weights):
+    half = (2, 16, BLK, BLK)
+    half_scale = (2, 16, 1, BLK)
     return pl.pallas_call(
         final_body,
-        in_specs=[ANY, VMEM],
-        out_specs=[ANY, VMEM],
+        in_specs=[ANY, ANY, ANY, VMEM],
+        out_specs=[ANY, ANY, VMEM],
         out_shape=[
-            jax.ShapeDtypeStruct((32,) + tile, F32),
+            jax.ShapeDtypeStruct((4, 16, BLK, BLK), I16),
+            jax.ShapeDtypeStruct((4, 16, 1, BLK), F32),
             jax.ShapeDtypeStruct(weights.shape, F32),
         ],
         scratch_shapes=[
-            pltpu.VMEM((128,) + tile, F32),
-            *scratch,
+            pltpu.VMEM(half, I16),
+            pltpu.VMEM(half_scale, F32),
+            pltpu.VMEM(half, F32),
+            pltpu.VMEM(half, I16),
+            pltpu.VMEM(half_scale, F32),
             pltpu.VMEM((4,) + weights.shape, F32),
             pltpu.VMEM((4, 4) + weights.shape, F32),
-            DMA((4,)),
-            DMA((8,)),
+            DMA((2,)),
             DMA((64,)),
             DMA((64,)),
         ],
         compiler_params=remote_params(2),
-    )(own, weights)
+    )(codes, scales, relay.reshape(half), weights)
+
+
+def total_body(
+    own, near, near_scale, relayed, relayed_scale, weights, factor,
+    out, w_self_out, w_neigh_out, bias_out,
+):
+    @pl.loop(0, own.shape[0], unroll=2)
+    def _(b):
+        others = decode(near[0, b], near_scale[0, b]) + decode(relayed[0, b], relayed_scale[0, b])
+        out[b] = own[b] + others
+
+    @pl.when(pl.program_id(0) == 0)
+    def _():
+        scale = factor[0]
+        w_self_out[...] = weights[0:128, :] * scale
+        w_neigh_out[...] = weights[128:256, :] * scale
+        bias_out[...] = weights[256:257, :] * scale
+
+
+def total(own, codes, scales, weights, factor):
+    def whole(*shape):
+        return pl.BlockSpec(shape, lambda i: (0,) * len(shape))
+
+    def message(number):
+        return [
+            pl.BlockSpec((1, 16, BLK, BLK), lambda i: (number(i), 0, 0, 0)),
+            pl.BlockSpec((1, 16, 1, BLK), lambda i: (number(i), 0, 0, 0)),
+        ]
+
+    half = pl.BlockSpec((16, BLK, BLK), lambda i: (i, 0, 0))
+    return pl.pallas_call(
+        total_body,
+        grid=(2,),
+        in_specs=[
+            half,
+            *message(lambda i: 1 - i),
+            *message(lambda i: 2 + i),
+            whole(264, BLK),
+            SMEM,
+        ],
+        out_specs=[half, whole(BLK, BLK), whole(BLK, BLK), whole(1, BLK)],
+        out_shape=[
+            jax.ShapeDtypeStruct((32, BLK, BLK), F32),
+            jax.ShapeDtypeStruct((BLK, BLK), F32),
+            jax.ShapeDtypeStruct((BLK, BLK), F32),
+            jax.ShapeDtypeStruct((1, BLK), F32),
+        ],
+        compiler_params=PARAMS,
+    )(own, codes, scales, codes, scales, weights, factor)
 
 
 def local(
@@ -924,7 +1067,7 @@
     )
     hub_grad, halo_grad, num_sum = owners(far, num)
     where = target_block * rows + z * (targets // 4)
-    own, layer, weights = settle(
+    own, relay, codes, scales, layer, weights = settle(
         idx,
         live,
         where,
@@ -939,15 +1082,12 @@
         w_neigh,
         out_bias[None, :],
     )
-    grad_features, weights = final(own.reshape(-1, BLK, feat), weights)
-    weights = weights / math.sqrt(targets * peers)
-    return (
-        layer,
-        grad_features.reshape(-1, feat),
-        weights[:feat],
-        weights[feat : 2 * feat],
-        weights[2 * feat],
+    codes, scales, weights = final(codes, scales, relay, weights)
+    factor = jnp.full((1,), 1.0 / math.sqrt(targets * peers), F32)
+    grad_features, self_grad, neigh_grad, bias_grad = total(
+        own.reshape(-1, BLK, feat), codes, scales, weights, factor
     )
+    return layer, grad_features.reshape(-1, feat), self_grad, neigh_grad, bias_grad[0]
 
 
 def solution(mesh):

time: 185 us -> 171 us (0.924)
  Pallas kernels: 167 us -> 158 us
  local copies, waits for them, and re-layouts: 11.8 us -> 7.56 us
    pallas_call x1, Pallas kernels: 43.5 us -> 30.1 us  [owners(): pl.pallas_call(owners_body, in_specs=[ANY, ANY], out_specs=[VMEM, VMEM, V...]
    pallas_call x1 -> x2, Pallas kernels: 45.9 us -> 50.8 us  [the longest x1 47.2 us: final(): pl.pallas_call(final_body, in_specs=[ANY, ANY, ANY, VMEM], out_specs=[ANY...]
    unnamed x8 -> x7, local copies, waits for them, and re-layouts: 4.27 us -> 1.23 us
where the time goes in v3:
time: 171 us
  Pallas kernels  158 us (92%)
  local copies, waits for them, and re-layouts  7.56 us (4%)
  other arithmetic  3.62 us (2%)
    pallas_call x1, Pallas kernels, final(): pl.pallas_call(final_body, in_specs=[ANY, ANY, ANY, VMEM], out_specs=[ANY...  47.2 us
    pallas_call x1, Pallas kernels, exchange(): pl.pallas_call(exchange_body, in_specs=[ANY, ANY, ANY], out_specs=[VMEM,...  33.3 us
    pallas_call x1, Pallas kernels, products(): pl.pallas_call(products_body, in_specs=[SMEM, ANY, VMEM, VMEM, VMEM, ANY,...  32.2 us
    pallas_call x1, Pallas kernels, owners(): pl.pallas_call(owners_body, in_specs=[ANY, ANY], out_specs=[VMEM, VMEM, V...  30.1 us
    pallas_call x1, Pallas kernels, settle(): pl.pallas_call(settle_body, in_specs=[SMEM, SMEM, SMEM, ANY, VMEM, VMEM,...  11.9 us
    gather x1, local copies, waits for them, and re-layouts, local(): picked = features[idx]  5.36 us
    pallas_call x1, Pallas kernels, total(): pl.pallas_call(total_body, grid=(2,), in_specs=[half, *message(lambda i:...  3.64 us

profile of v3, /device:TPU:0, one launch (start us, length us, event | category | flops | bytes accessed | tf_op | source)
XLA Modules:
  0.0 170.9 jit_solution(5080786834645229892)
XLA Ops:
  0.6 0.0 copy-start
  0.7 0.7 copy-done
  1.4 0.7 fusion
  2.1 5.4 %gather_fusion = bf16[1536,128]{1,0:T(8,128)(2,1)S(1)} fusion(bf16[16384,128]{1,0:T(8,128)(2,1)} %feats.1, s32[2048]{0:T(1024)S(1)} %pad_clamp_fusion), kind=kCustom, calls=%fused_computation | custom fusion | bytes 792576 | tf_op jit(solution)/shard_map/gather | solution.py:1051
  7.5 0.5 broadcast.38
  8.0 1.3 reduce.7
  9.3 0.1 reshape_squeeze.7
  9.4 0.2 dynamic-slice_reduce_fusion.live
  9.6 0.0 copy-start.2
  9.6 0.1 iota_compare_fusion
  9.7 0.9 broadcast_select_fusion.halo_in
  10.6 0.7 slice.10
  11.2 33.3 %shard_map.146 = (f32[16,128]{1,0:T(8,128)}, bf16[4,4,2,2,256,128]{5,4,3,2,1,0:T(8,128)(2,1)}, bf16[8,4,128,128]{3,2,1,0:T(8,128)(2,1)}) custom-call(bf16[16,128,32,128]{3,2,1,0:T(8,128)(2,1)} %bitcast.25, bf16[2,256,128]{2,1,0:T(8,128)(2,1)} %bitcast.36, bf16[8,128,128]{2,1,0:T(8,128)(2,1)} %broadcast_select_fusion.halo_in), custom_call_target="tpu_custom_call" | custom-call | tf_op jit(solution)/shard_map/pallas_call | solution.py:276
  44.5 0.0 copy-done.2
  44.5 32.2 %shard_map.147 = (f32[128,128,128]{2,1,0:T(8,128)}, f32[160,128,128]{2,1,0:T(8,128)}, f32[2048,128]{1,0:T(8,128)}) custom-call(s32[16,32]{1,0:T(8,128)} %bitcast.39, bf16[16,128,32,128]{3,2,1,0:T(8,128)(2,1)} %bitcast.26, bf16[2048,128]{1,0:T(8,128)(2,1)} %grads.3, bf16[128,128]{1,0:T(8,128)(2,1)} %w_neigh.3, f32[16,128]{1,0:T(8,128)} %get-tuple-element.27.deg, ...), custom_call_target="tpu_custom_call" | custom-call | tf_op jit(solution)/shard_map/pallas_call | solution.py:379
  76.7 0.0 copy-start.1
  76.7 30.1 %shard_map.148 = (f32[4,128,128]{2,1,0:T(8,128)}, f32[8,128,128]{2,1,0:T(8,128)}, f32[4,128,128]{2,1,0:T(8,128)}) custom-call(f32[160,128,128]{2,1,0:T(8,128)} %get-tuple-element.31.far, f32[16,128,128]{2,1,0:T(8,128)} %bitcast.34), custom_call_target="tpu_custom_call" | custom-call | tf_op jit(solution)/shard_map/pallas_call | solution.py:694
  106.8 0.0 copy-done.1
  106.8 0.6 pad_add_fusion.idx
  108.1 11.9 %shard_map.149 = (f32[4096,128]{1,0:T(8,128)}, f32[2,2048,128]{2,1,0:T(8,128)}, s16[4,16,128,128]{3,2,1,0:T(8,128)(2,1)}, f32[4,16,1,128]{3,2,1,0:T(1,128)}, bf1...) custom-call(s32[1536]{0:T(1024)} %pad_add_fusion.idx, s32[8]{0:T(128)} %copy-done.2, s32[1]{0:T(128)S(6)} %add.31.where, ...), custom_call_target="tpu_custom_call" | custom-call | tf_op jit(solution)/shard_map/pallas_call | solution.py:835
  120.0 47.2 %shard_map.150 = (s16[4,16,128,128]{3,2,1,0:T(8,128)(2,1)}, f32[4,16,1,128]{3,2,1,0:T(1,128)}, f32[264,128]{1,0:T(8,128)}) custom-call(s16[4,16,128,128]{3,2,1,0:T(8,128)(2,1)} %get-tuple-element.38.codes, f32[4,16,1,128]{3,2,1,0:T(1,128)} %get-tuple-element.39.scales, f32[2,16,128,128]{3,2,1,0:T(8,128)} %bitcast.31, f32[264,128]{1,0:T(8,128)} %get-tuple-element.41.weights), custom_call_target="tpu_custom_call" | custom-call | tf_op jit(solution)/shard_map/pallas_call | solution.py:949
  167.1 3.6 %shard_map.151 = (f32[32,128,128]{2,1,0:T(8,128)}, f32[128,128]{1,0:T(8,128)}, f32[128,128]{1,0:T(8,128)}, f32[1,128]{1,0:T(1,128)}) custom-call(f32[32,128,128]{2,1,0:T(8,128)} %bitcast.30, s16[4,16,128,128]{3,2,1,0:T(8,128)(2,1)} %get-tuple-element.42.near.relayed, f32[4,16,1,128]{3,2,1,0:T(1,128)} %get-tuple-element.43.near_scale.relayed_scale, ...), custom_call_target="tpu_custom_call" | custom-call | tf_op jit(solution)/shard_map/pallas_call | solution.py:1002
  (4 shorter events, 0.0 us)
Async XLA Ops:
  0.6 0.7 copy-start
  9.6 34.9 %copy-start.2 = (s32[8]{0:T(128)}, s32[8]{0:T(128)S(1)}, u32[]{:S(2)}) copy-start(s32[8]{0:T(128)S(1)} %dynamic-slice_reduce_fusion.live) | copy-start | bytes 100
  76.7 30.1 %copy-start.1 = (s32[1,512]{1,0:T(1,128)S(1)}, s32[1,512]{1,0:T(1,128)}, u32[]{:S(2)}) copy-start(s32[1,512]{1,0:T(1,128)} %param.14) | copy-start | bytes 6148

commit v4 on v3

--- a/solution.py
+++ b/solution.py
@@ -1,3 +1,4 @@
+import functools
 import math
 
 import jax
@@ -122,8 +123,9 @@
 
 
 def exchange_body(
-    adj, hub_in, halo_in, deg_out, hub_out, halo_out,
-    buf, deg_all, deg_mine, adj_sem, local_sem, send_sem, recv_sem, far_send, far_recv,
+    hub_idx, list_idx, live, adj, feats, deg_out, hub_out, halo_out,
+    buf, packed, wide, picked, hub_in, halo_in, deg_all, deg_mine,
+    feat_sem, adj_sem, local_sem, send_sem, recv_sem, far_send, far_recv,
 ):
     place = Place()
     x, y, c, d, z = place.x, place.y, place.core, place.d, place.z
@@ -131,11 +133,41 @@
     blocks = adj.shape[0]
     near = [("x", 1), ("x", -1), ("y", 1), ("y", -1), ("z", 1), ("z", -1), ("z", 2), ("core", 1)]
     ready = greet(place, near, far=True)
+    span = feats.shape[0] // 4
+    feat_copies = []
+    for g in range(4):
+        part = pl.ds(g * span, span)
+        feat_copies.append(pltpu.make_async_copy(feats.at[part], packed.at[part], feat_sem.at[g]))
+        feat_copies[-1].start()
     for b in range(blocks):
         block_copy(adj, buf, adj_sem, b).start()
+    links = Links(send_sem, recv_sem)
+    for g in range(4):
+        feat_copies[g].wait()
+
+        @pl.loop(g * span // 128, (g + 1) * span // 128, unroll=2)
+        def _(i):
+            part = pl.ds(pl.multiple_of(i * 128, 128), 128)
+            wide[part, :] = packed[part, :].astype(F32)
+
+    def pick(place_of, store):
+        @pl.loop(0, 8)
+        def _(g):
+            for i in range(16):
+                picked[pl.ds(g * 16 + i, 1), :] = wide[pl.ds(place_of(g * 16 + i), 1), :]
+
+        store(picked[...])
+
+    for half in range(2):
+        for part in range(2):
+            base = (half * 2 + part) * 128
+
+            def store(rows, half=half, part=part):
+                hub_in[half, pl.ds(part * 128, 128), :] = rows.astype(BF16)
+
+            pick(lambda i, base=base: hub_idx[base + i], store)
     own_hub = pltpu.make_async_copy(hub_in, hub_out.at[y, x, c], local_sem.at[0])
     own_hub.start()
-    links = Links(send_sem, recv_sem)
 
     def degrees(low, high):
         @pl.loop(low, high)
@@ -169,7 +201,6 @@
         cores.append(pass_on(ref, "core", 1))
 
     first, relay, second, third = {}, {}, {}, {}
-    degrees(0, 1)
     ready()
     for flow in flows:
         axis, other, half = flow
@@ -177,27 +208,33 @@
             first[axis, by] = links.send(
                 hub_in.at[half], piece(flow, 0, 0), place.device(axis, by)
             )
-    here = lax.div(d, 4)
-    for j in range(8):
-
-        @pl.when(j * 4 + share != d)
-        def _():
-            there = halo_out.at[here, lax.rem(d, 4)]
-            peer_copy(place, halo_in.at[j], there, j, far_send, far_recv, True).start()
-
-        @pl.when(j * 4 + share == d)
-        def _():
-            keep = pltpu.make_async_copy(halo_in.at[j], halo_out.at[j, share], local_sem.at[1])
-            keep.start()
-            keep.wait()
-
     for flow in flows:
         axis, other, half = flow
         for by in (1, -1):
             second[axis, 0, by] = links.send(
                 hub_in.at[half], piece(flow, 0, 0), place.device(other, by)
             )
-    degrees(1, 4)
+    here = lax.div(d, 4)
+    for j in range(8):
+
+        def store(rows, j=j):
+            slot = lax.broadcasted_iota(I32, rows.shape, 0)
+            halo_in[j] = jnp.where(slot < live[j * 4 + share], rows, 0.0).astype(BF16)
+
+        pick(lambda i, j=j: list_idx[j * 4 + share, i], store)
+
+        @pl.when(j * 4 + share != d)
+        def _():
+            there = halo_out.at[here, lax.rem(d, 4)]
+            peer_copy(place, halo_in.at[j], there, j, far_send, far_recv, True).start()
+
+        @pl.when(j * 4 + share == d)
+        def _():
+            keep = pltpu.make_async_copy(halo_in.at[j], halo_out.at[j, share], local_sem.at[1])
+            keep.start()
+            keep.wait()
+
+    degrees(0, 4)
     own_hub.wait()
     for flow in flows:
         to_core(piece(flow, 0, 0))
@@ -270,22 +307,29 @@
     links.drain()
 
 
-def exchange(adj, hub_in, halo_in):
+def exchange(adj, feats, hub_idx, list_idx, live):
     blocks, rows, _, _ = adj.shape
-    hubs, feat = hub_in.shape
+    hubs, feat = hub_idx.shape[0], feats.shape[1]
+    slots = list_idx.shape[1]
     return pl.pallas_call(
         exchange_body,
-        in_specs=[ANY, ANY, ANY],
+        in_specs=[SMEM, SMEM, SMEM, ANY, ANY],
         out_specs=[VMEM, ANY, ANY],
         out_shape=[
             jax.ShapeDtypeStruct((blocks, rows), F32),
             jax.ShapeDtypeStruct((4, 4, 2, 2, hubs // 2, feat), BF16),
-            jax.ShapeDtypeStruct((8, 4) + halo_in.shape[1:], BF16),
+            jax.ShapeDtypeStruct((8, 4, slots, feat), BF16),
         ],
         scratch_shapes=[
             pltpu.VMEM(adj.shape, BF16),
+            pltpu.VMEM(feats.shape, BF16),
+            pltpu.VMEM(feats.shape, F32),
+            pltpu.VMEM((128, feat), F32),
+            pltpu.VMEM((2, hubs // 2, feat), BF16),
+            pltpu.VMEM((8, slots, feat), BF16),
             pltpu.VMEM((4, blocks, rows), F32),
             pltpu.VMEM((blocks, rows), F32),
+            DMA((4,)),
             DMA((blocks,)),
             DMA((2,)),
             DMA((96,)),
@@ -294,7 +338,7 @@
             DMA((8,)),
         ],
         compiler_params=remote_params(0),
-    )(adj, hub_in.reshape(2, hubs // 2, feat), halo_in)
+    )(hub_idx, list_idx, live, adj, feats)
 
 
 def split_slots(tiles, adj_block):
@@ -735,24 +779,25 @@
 
 
 def settle_body(
-    idx, live, where, own, hub, halo, num, deg, feats, grads, w_self, w_neigh, bias,
+    hub_idx, list_idx, live, target, own, hub, halo, num, deg, feats, grads, w_self, w_neigh, bias,
     own_out, relay_out, codes, scales, layer, weights, table, self_rows, code, scale, sem, out_sem,
 ):
     share = lax.axis_index("esplit")
+    lists = Place().share()
     step = own.shape[0] // 4
+    first = pl.multiple_of(target[0] * 128 + share * 512, 128)
+    own_rows = pltpu.make_async_copy(feats.at[pl.ds(first, 512)], self_rows, sem.at[4])
+    own_rows.start()
     loads = []
     for g in range(4):
         part = pl.ds(g * step, step)
         loads.append(pltpu.make_async_copy(own.at[part], table.at[part], sem.at[g]))
-    first = pl.multiple_of(where[0], 128)
-    loads.append(pltpu.make_async_copy(feats.at[pl.ds(first, 512)], self_rows, sem.at[4]))
-    for load in loads:
-        load.start()
+        loads[-1].start()
 
     at = pl.multiple_of(share * 512, 512)
     my_grads = grads[pl.ds(at, 512), :]
     wide = my_grads.astype(F32)
-    loads[4].wait()
+    own_rows.wait()
     mine = self_rows[...]
     contract = (((0,), (0,)), ((), ()))
     weights[0:128, :] = lax.dot_general(mine, my_grads, contract, preferred_element_type=F32)
@@ -777,31 +822,34 @@
         )
     weights[128:256, :] = neigh
     weights[256:264, :] = jnp.broadcast_to(jnp.sum(wide, axis=0, keepdims=True), (8, 128))
+    weights[264:288, :] = jnp.zeros((24, 128), F32)
     for j in range(8):
         row = lax.broadcasted_iota(I32, (128, 128), 0)
         halo[pl.ds(j * 128, 128), :] = jnp.where(
-            row < live[j], halo[pl.ds(j * 128, 128), :], 0.0
+            row < live[j * 4 + lists], halo[pl.ds(j * 128, 128), :], 0.0
         )
     back = lax.dot_general(
         my_grads, w_self[...], (((1,), (1,)), ((), ())), preferred_element_type=F32
     )
-    for load in loads[:4]:
+    for load in loads:
         load.wait()
     table[pl.ds(first, 512), :] += back
 
-    def scatter(rows, base, count):
-        @pl.loop(0, count // 8)
+    def scatter(rows, place_of, count):
+        @pl.loop(0, count // 8, unroll=2)
         def _(g):
-            places = [idx[base + g * 8 + i] for i in range(8)]
+            places = [place_of(g * 8 + i) for i in range(8)]
             values = [
                 table[pl.ds(places[i], 1), :] + rows[pl.ds(g * 8 + i, 1), :] for i in range(8)
             ]
             for i in range(8):
                 table[pl.ds(places[i], 1), :] = values[i]
 
-    scatter(hub, 0, 512)
+    scatter(hub, lambda i: hub_idx[i], 512)
     for j in range(8):
-        scatter(halo.at[pl.ds(j * 128, 128)], 512 + j * 128, 128)
+        scatter(
+            halo.at[pl.ds(j * 128, 128)], lambda i, j=j: list_idx[j * 4 + lists, i], 128
+        )
     outs = []
 
     def put(src, dst):
@@ -829,12 +877,12 @@
         out.wait()
 
 
-def settle(idx, live, where, own, hub, halo, num, deg, feats, grads, w_self, w_neigh, bias):
+def settle(hub_idx, list_idx, live, target, own, hub, halo, num, deg, feats, grads, w_self, w_neigh, bias):
     codes = (4, 16, BLK, BLK)
     scales = (4, 16, 1, BLK)
     return pl.pallas_call(
         settle_body,
-        in_specs=[SMEM, SMEM, SMEM, ANY, VMEM, VMEM, VMEM, VMEM, ANY, VMEM, VMEM, VMEM, VMEM],
+        in_specs=[SMEM, SMEM, SMEM, SMEM, ANY, VMEM, VMEM, VMEM, VMEM, ANY, VMEM, VMEM, VMEM, VMEM],
         out_specs=[ANY, ANY, ANY, ANY, VMEM, VMEM],
         out_shape=[
             jax.ShapeDtypeStruct((4096, 128), F32),
@@ -842,7 +890,7 @@
             jax.ShapeDtypeStruct(codes, I16),
             jax.ShapeDtypeStruct(scales, F32),
             jax.ShapeDtypeStruct((512, 128), BF16),
-            jax.ShapeDtypeStruct((264, 128), F32),
+            jax.ShapeDtypeStruct((288, 128), F32),
         ],
         scratch_shapes=[
             pltpu.VMEM(own.shape, F32),
@@ -853,12 +901,12 @@
             DMA((11,)),
         ],
         compiler_params=PARAMS,
-    )(idx, live, where, own, hub, halo, num, deg, feats, grads, w_self, w_neigh, bias)
+    )(hub_idx, list_idx, live, target, own, hub, halo, num, deg, feats, grads, w_self, w_neigh, bias)
 
 
 def final_body(
     codes, scales, relay_in, weights, come, come_scale, weights_out,
-    far, far_scale, part, out, out_scale, sums, slots, load_sem, send_sem, recv_sem,
+    far, far_scale, part, out, out_scale, slots, line, load_sem, send_sem, recv_sem,
 ):
     place = Place()
     links = Links(send_sem, recv_sem)
@@ -887,14 +935,31 @@
                 far.at[m, quad[g]], far_scale.at[m, quad[g]],
             )
 
+    x = place.x
+    held = {}
+
+    def scatter_sum():
+        rounds = [
+            links.send(weights.at[place.step("x", by)], slots.at[0, x], place.device("x", by))
+            for by in (1, -1, 2)
+        ]
+        slots[0, x] = weights[x]
+
+        def end():
+            for copy in rounds:
+                copy.wait_recv()
+            held[0] = (slots[0, 0] + slots[0, 1]) + (slots[0, 2] + slots[0, 3])
+
+        return end
+
     def all_sum(stage, axis):
         mine = place.core if axis == "core" else place.at(axis)
-        there = [1] if axis == "core" else [1, -1, 2]
+        line[stage - 1] = held[0]
         rounds = [
-            links.send(sums.at[stage], slots.at[stage, mine], place.device(axis, by))
-            for by in there
+            links.send(line.at[stage - 1], slots.at[stage, mine], place.device(axis, by))
+            for by in ([1] if axis == "core" else [1, -1, 2])
         ]
-        slots[stage, mine] = sums[stage]
+        slots[stage, mine] = held[0]
 
         def end():
             for copy in rounds:
@@ -902,15 +967,24 @@
             total = slots[stage, 0] + slots[stage, 1]
             if axis != "core":
                 total = total + (slots[stage, 2] + slots[stage, 3])
-            if stage == 3:
-                weights_out[...] = total
-            else:
-                sums[stage + 1] = total
+            held[0] = total
 
         return end
 
-    sums[0] = weights[...]
-    end = all_sum(0, "core")
+    def gather_parts():
+        line[3] = held[0]
+        rounds = [
+            links.send(line.at[3], weights_out.at[x], place.device("x", by)) for by in (1, -1, 2)
+        ]
+        weights_out[x] = held[0]
+
+        def end():
+            for copy in rounds:
+                copy.wait_recv()
+
+        return end
+
+    end = scatter_sum()
     for g in range(4):
         for m in (2, 3):
             copies[m, g] = send(
@@ -935,7 +1009,10 @@
             )
         end()
         if g < 3:
-            end = all_sum(g + 1, ("x", "y", "z")[g])
+            end = all_sum(g + 1, ("y", "core", "z")[g])
+        else:
+            end = gather_parts()
+    end()
     for m in (2, 3, 4, 5):
         for g in range(4):
             for copy in copies[m, g]:
@@ -962,7 +1039,7 @@
             pltpu.VMEM(half, I16),
             pltpu.VMEM(half_scale, F32),
             pltpu.VMEM((4,) + weights.shape, F32),
-            pltpu.VMEM((4, 4) + weights.shape, F32),
+            pltpu.VMEM(weights.shape, F32),
             DMA((2,)),
             DMA((64,)),
             DMA((64,)),
@@ -972,7 +1049,7 @@
 
 
 def total_body(
-    own, near, near_scale, relayed, relayed_scale, weights, factor,
+    factor, own, near, near_scale, relayed, relayed_scale, weights,
     out, w_self_out, w_neigh_out, bias_out,
 ):
     @pl.loop(0, own.shape[0], unroll=2)
@@ -982,10 +1059,9 @@
 
     @pl.when(pl.program_id(0) == 0)
     def _():
-        scale = factor[0]
-        w_self_out[...] = weights[0:128, :] * scale
-        w_neigh_out[...] = weights[128:256, :] * scale
-        bias_out[...] = weights[256:257, :] * scale
+        w_self_out[...] = weights[0:128, :] * factor
+        w_neigh_out[...] = weights[128:256, :] * factor
+        bias_out[...] = weights[256:257, :] * factor
 
 
 def total(own, codes, scales, weights, factor):
@@ -1000,14 +1076,13 @@
 
     half = pl.BlockSpec((16, BLK, BLK), lambda i: (i, 0, 0))
     return pl.pallas_call(
-        total_body,
+        functools.partial(total_body, factor),
         grid=(2,),
         in_specs=[
             half,
             *message(lambda i: 1 - i),
             *message(lambda i: 2 + i),
-            whole(264, BLK),
-            SMEM,
+            whole(288, BLK),
         ],
         out_specs=[half, whole(BLK, BLK), whole(BLK, BLK), whole(1, BLK)],
         out_shape=[
@@ -1017,7 +1092,7 @@
             jax.ShapeDtypeStruct((1, BLK), F32),
         ],
         compiler_params=PARAMS,
-    )(own, codes, scales, codes, scales, weights, factor)
+    )(own, codes, scales, codes, scales, weights)
 
 
 def local(
@@ -1035,26 +1110,12 @@
 ):
     own_count, feat = features.shape
     peers = lax.axis_size("dom")
-    d = lax.axis_index("dom")
-    z = lax.axis_index("esplit")
     adj = adjacency[0, 0]
     src = tile_source[0, 0]
     blocks, rows, _, cols = adj.shape
     targets = blocks * rows
-    hub_idx = hub_rows[0]
-    hubs = hub_idx.shape[0]
-    share = lax.rem(z - d + peers, 4)
-    slots = send_rows.shape[2]
-    lists = lax.dynamic_index_in_dim(send_rows[0].reshape(8, 4, slots), share, 1, keepdims=False)
-    live = lax.dynamic_index_in_dim(send_live[0].reshape(8, 4), share, 1, keepdims=False)
-    idx = jnp.concatenate([hub_idx, lists.reshape(-1)])
-    picked = features[idx]
-    hub_local = picked[:hubs]
-    alive = jnp.arange(slots, dtype=I32)[None, :] < live[:, None]
-    halo_local = jnp.where(
-        alive[:, :, None], picked[hubs:].reshape(8, slots, feat), jnp.zeros((), features.dtype)
-    )
-    deg, hub_all, halo_all = exchange(adj, hub_local, halo_local)
+    hub_idx, list_idx, live = hub_rows[0], send_rows[0], send_live[0]
+    deg, hub_all, halo_all = exchange(adj, features, hub_idx, list_idx, live)
     own, far, num = products(
         src,
         adj,
@@ -1066,11 +1127,11 @@
         halo_all.reshape(-1, cols, feat),
     )
     hub_grad, halo_grad, num_sum = owners(far, num)
-    where = target_block * rows + z * (targets // 4)
     own, relay, codes, scales, layer, weights = settle(
-        idx,
+        hub_idx,
+        list_idx,
         live,
-        where,
+        target_block,
         own.reshape(-1, feat),
         hub_grad.reshape(-1, feat),
         halo_grad.reshape(-1, feat),
@@ -1082,8 +1143,9 @@
         w_neigh,
         out_bias[None, :],
     )
-    codes, scales, weights = final(codes, scales, relay, weights)
-    factor = jnp.full((1,), 1.0 / math.sqrt(targets * peers), F32)
+    codes, scales, weights = final(codes, scales, relay, weights.reshape(4, 72, feat))
+    weights = weights.reshape(-1, feat)
+    factor = 1.0 / math.sqrt(targets * peers)
     grad_features, self_grad, neigh_grad, bias_grad = total(
         own.reshape(-1, BLK, feat), codes, scales, weights, factor
     )

time: 171 us -> 163 us (0.953)
  local copies, waits for them, and re-layouts: 7.56 us -> 0 us
  other arithmetic: 3.62 us -> 0 us
  Pallas kernels: 158 us -> 161 us
    gather x1 -> x0, local copies, waits for them, and re-layouts: 5.36 us -> none  [local(): picked = features[idx]]
    pallas_call x3, Pallas kernels: 48.8 us -> 52.7 us  [the longest x1 37.1 us: exchange(): pl.pallas_call(exchange_body, in_specs=[SMEM, SMEM, SMEM, ANY, ANY], out_...]
    pallas_call x1, Pallas kernels: 47.2 us -> 45.4 us  [final(): pl.pallas_call(final_body, in_specs=[ANY, ANY, ANY, VMEM], out_specs=[ANY...]
where the time goes in v4:
time: 163 us
  Pallas kernels  161 us (99%)
    pallas_call x1, Pallas kernels, final(): pl.pallas_call(final_body, in_specs=[ANY, ANY, ANY, VMEM], out_specs=[ANY...  45.4 us
    pallas_call x1, Pallas kernels, exchange(): pl.pallas_call(exchange_body, in_specs=[SMEM, SMEM, SMEM, ANY, ANY], out_...  37.1 us
    pallas_call x1, Pallas kernels, products(): pl.pallas_call(products_body, in_specs=[SMEM, ANY, VMEM, VMEM, VMEM, ANY,...  32.2 us
    pallas_call x1, Pallas kernels, owners(): pl.pallas_call(owners_body, in_specs=[ANY, ANY], out_specs=[VMEM, VMEM, V...  31 us
    pallas_call x1, Pallas kernels, settle(): pl.pallas_call(settle_body, in_specs=[SMEM, SMEM, SMEM, SMEM, ANY, VMEM,...  11.9 us
    pallas_call x1, Pallas kernels, total(): pl.pallas_call(functools.partial(total_body, factor), grid=(2,), in_specs...  3.64 us

profile of v4, /device:TPU:0, one launch (start us, length us, event | category | flops | bytes accessed | tf_op | source)
XLA Modules:
  0.0 162.5 jit_solution(12946064453761527873)
XLA Ops:
  0.6 37.1 %shard_map.146 = (f32[16,128]{1,0:T(8,128)}, bf16[4,4,2,2,256,128]{5,4,3,2,1,0:T(8,128)(2,1)}, bf16[8,4,128,128]{3,2,1,0:T(8,128)(2,1)}) custom-call(s32[512]{0:T(512)} %bitcast.35, s32[32,128]{1,0:T(8,128)} %bitcast.32, s32[32]{0:T(128)} %bitcast.37, bf16[16,128,32,128]{3,2,1,0:T(8,128)(2,1)} %bitcast.19, bf16[16384,128]{1,0:T(8,128)(2,1)} %feats.3), custom_call_target="tpu_custom_call" | custom-call | tf_op jit(solution)/shard_map/pallas_call | solution.py:314
  37.8 32.2 %shard_map.147 = (f32[128,128,128]{2,1,0:T(8,128)}, f32[160,128,128]{2,1,0:T(8,128)}, f32[2048,128]{1,0:T(8,128)}) custom-call(s32[16,32]{1,0:T(8,128)} %bitcast.34, bf16[16,128,32,128]{3,2,1,0:T(8,128)(2,1)} %bitcast.20, bf16[2048,128]{1,0:T(8,128)(2,1)} %grads.3, bf16[128,128]{1,0:T(8,128)(2,1)} %w_neigh.3, f32[16,128]{1,0:T(8,128)} %get-tuple-element.27.deg, ...), custom_call_target="tpu_custom_call" | custom-call | tf_op jit(solution)/shard_map/pallas_call | solution.py:423
  69.9 31.0 %shard_map.148 = (f32[4,128,128]{2,1,0:T(8,128)}, f32[8,128,128]{2,1,0:T(8,128)}, f32[4,128,128]{2,1,0:T(8,128)}) custom-call(f32[160,128,128]{2,1,0:T(8,128)} %get-tuple-element.31.far, f32[16,128,128]{2,1,0:T(8,128)} %bitcast.27), custom_call_target="tpu_custom_call" | custom-call | tf_op jit(solution)/shard_map/pallas_call | solution.py:738
  101.6 11.9 %shard_map.149 = (f32[4096,128]{1,0:T(8,128)}, f32[2,2048,128]{2,1,0:T(8,128)}, s16[4,16,128,128]{3,2,1,0:T(8,128)(2,1)}, f32[4,16,1,128]{3,2,1,0:T(1,128)}, bf1...) custom-call(s32[512]{0:T(512)} %bitcast.36, s32[32,128]{1,0:T(8,128)} %bitcast.33, s32[32]{0:T(128)} %bitcast.38, ...), custom_call_target="tpu_custom_call" | custom-call | tf_op jit(solution)/shard_map/pallas_call | solution.py:883
  113.5 45.4 %shard_map.150 = (s16[4,16,128,128]{3,2,1,0:T(8,128)(2,1)}, f32[4,16,1,128]{3,2,1,0:T(1,128)}, f32[4,72,128]{2,1,0:T(8,128)}) custom-call(s16[4,16,128,128]{3,2,1,0:T(8,128)(2,1)} %get-tuple-element.38.codes, f32[4,16,1,128]{3,2,1,0:T(1,128)} %get-tuple-element.39.scales, f32[2,16,128,128]{3,2,1,0:T(8,128)} %bitcast.25, f32[4,72,128]{2,1,0:T(8,128)} %bitcast.30), custom_call_target="tpu_custom_call" | custom-call | tf_op jit(solution)/shard_map/pallas_call | solution.py:1026
  158.9 3.6 %shard_map.151 = (f32[32,128,128]{2,1,0:T(8,128)}, f32[128,128]{1,0:T(8,128)}, f32[128,128]{1,0:T(8,128)}, f32[1,128]{1,0:T(1,128)}) custom-call(f32[32,128,128]{2,1,0:T(8,128)} %bitcast.24, s16[4,16,128,128]{3,2,1,0:T(8,128)(2,1)} %get-tuple-element.42.near.relayed, f32[4,16,1,128]{3,2,1,0:T(1,128)} %get-tuple-element.43.near_scale.relayed_scale, ...), custom_call_target="tpu_custom_call" | custom-call | tf_op jit(solution)/shard_map/pallas_call | solution.py:1078

commit v5 on v4

--- a/solution.py
+++ b/solution.py
@@ -287,14 +287,14 @@
     for along in (-1, 1):
         for flow in flows:
             carry(flow, along)
+    for flow in flows:
+        carry(flow, 2)
     for j in range(8):
         for by in (1, -1):
             halo_first[j, by].wait_recv()
             if (by == 1) == (j % 2 == 0):
                 back = lax.rem(place.step("z", -by) - d + 32, 4)
                 halo_relay.append(pass_on(halo_out.at[j, back], "z", by))
-    for flow in flows:
-        carry(flow, 2)
     for along in (0, -1, 1, 2):
         for flow in flows:
             third[flow[0], along].wait_recv()
@@ -352,8 +352,6 @@
     table, rows_in, buf, tiles, sem, in_sem, out_sem,
 ):
     blocks, rows, slots, _ = adj.shape
-    for b in range(blocks):
-        block_copy(adj, buf, sem, b).start()
     copies = []
     start = 0
     for i, part in enumerate((own, hub, halo)):
@@ -362,6 +360,8 @@
         start += count
     for copy in copies:
         copy.start()
+    for b in range(blocks):
+        block_copy(adj, buf, sem, b).start()
 
     @pl.loop(0, table.shape[0], unroll=8)
     def _(c):

time: 163 us -> 163 us (level)
  no operation moved by 1% of the time
where the time goes in v5:
time: 163 us; the launch traced here: 162 us
  Pallas kernels  161 us (99%)
    pallas_call x1, Pallas kernels, final(): pl.pallas_call(final_body, in_specs=[ANY, ANY, ANY, VMEM], out_specs=[ANY...  45.4 us
    pallas_call x1, Pallas kernels, exchange(): pl.pallas_call(exchange_body, in_specs=[SMEM, SMEM, SMEM, ANY, ANY], out_...  37.7 us
    pallas_call x1, Pallas kernels, products(): pl.pallas_call(products_body, in_specs=[SMEM, ANY, VMEM, VMEM, VMEM, ANY,...  31.9 us
    pallas_call x1, Pallas kernels, owners(): pl.pallas_call(owners_body, in_specs=[ANY, ANY], out_specs=[VMEM, VMEM, V...  30.4 us
    pallas_call x1, Pallas kernels, settle(): pl.pallas_call(settle_body, in_specs=[SMEM, SMEM, SMEM, SMEM, ANY, VMEM,...  11.9 us
    pallas_call x1, Pallas kernels, total(): pl.pallas_call(functools.partial(total_body, factor), grid=(2,), in_specs...  3.64 us

profile of v5, /device:TPU:0, one launch (start us, length us, event | category | flops | bytes accessed | tf_op | source)
XLA Modules:
  0.0 162.2 jit_solution(1176086983620672031)
XLA Ops:
  0.6 37.7 %shard_map.146 = (f32[16,128]{1,0:T(8,128)}, bf16[4,4,2,2,256,128]{5,4,3,2,1,0:T(8,128)(2,1)}, bf16[8,4,128,128]{3,2,1,0:T(8,128)(2,1)}) custom-call(s32[512]{0:T(512)} %bitcast.35, s32[32,128]{1,0:T(8,128)} %bitcast.32, s32[32]{0:T(128)} %bitcast.37, bf16[16,128,32,128]{3,2,1,0:T(8,128)(2,1)} %bitcast.19, bf16[16384,128]{1,0:T(8,128)(2,1)} %feats.3), custom_call_target="tpu_custom_call" | custom-call | tf_op jit(solution)/shard_map/pallas_call | solution.py:314
  38.3 31.9 %shard_map.147 = (f32[128,128,128]{2,1,0:T(8,128)}, f32[160,128,128]{2,1,0:T(8,128)}, f32[2048,128]{1,0:T(8,128)}) custom-call(s32[16,32]{1,0:T(8,128)} %bitcast.34, bf16[16,128,32,128]{3,2,1,0:T(8,128)(2,1)} %bitcast.20, bf16[2048,128]{1,0:T(8,128)(2,1)} %grads.3, bf16[128,128]{1,0:T(8,128)(2,1)} %w_neigh.3, f32[16,128]{1,0:T(8,128)} %get-tuple-element.27.deg, ...), custom_call_target="tpu_custom_call" | custom-call | tf_op jit(solution)/shard_map/pallas_call | solution.py:423
  70.2 30.4 %shard_map.148 = (f32[4,128,128]{2,1,0:T(8,128)}, f32[8,128,128]{2,1,0:T(8,128)}, f32[4,128,128]{2,1,0:T(8,128)}) custom-call(f32[160,128,128]{2,1,0:T(8,128)} %get-tuple-element.31.far, f32[16,128,128]{2,1,0:T(8,128)} %bitcast.27), custom_call_target="tpu_custom_call" | custom-call | tf_op jit(solution)/shard_map/pallas_call | solution.py:738
  101.3 11.9 %shard_map.149 = (f32[4096,128]{1,0:T(8,128)}, f32[2,2048,128]{2,1,0:T(8,128)}, s16[4,16,128,128]{3,2,1,0:T(8,128)(2,1)}, f32[4,16,1,128]{3,2,1,0:T(1,128)}, bf1...) custom-call(s32[512]{0:T(512)} %bitcast.36, s32[32,128]{1,0:T(8,128)} %bitcast.33, s32[32]{0:T(128)} %bitcast.38, ...), custom_call_target="tpu_custom_call" | custom-call | tf_op jit(solution)/shard_map/pallas_call | solution.py:883
  113.2 45.4 %shard_map.150 = (s16[4,16,128,128]{3,2,1,0:T(8,128)(2,1)}, f32[4,16,1,128]{3,2,1,0:T(1,128)}, f32[4,72,128]{2,1,0:T(8,128)}) custom-call(s16[4,16,128,128]{3,2,1,0:T(8,128)(2,1)} %get-tuple-element.38.codes, f32[4,16,1,128]{3,2,1,0:T(1,128)} %get-tuple-element.39.scales, f32[2,16,128,128]{3,2,1,0:T(8,128)} %bitcast.25, f32[4,72,128]{2,1,0:T(8,128)} %bitcast.30), custom_call_target="tpu_custom_call" | custom-call | tf_op jit(solution)/shard_map/pallas_call | solution.py:1026
  158.6 3.6 %shard_map.151 = (f32[32,128,128]{2,1,0:T(8,128)}, f32[128,128]{1,0:T(8,128)}, f32[128,128]{1,0:T(8,128)}, f32[1,128]{1,0:T(1,128)}) custom-call(f32[32,128,128]{2,1,0:T(8,128)} %bitcast.24, s16[4,16,128,128]{3,2,1,0:T(8,128)(2,1)} %get-tuple-element.42.near.relayed, f32[4,16,1,128]{3,2,1,0:T(1,128)} %get-tuple-element.43.near_scale.relayed_scale, ...), custom_call_target="tpu_custom_call" | custom-call | tf_op jit(solution)/shard_map/pallas_call | solution.py:1078
